TPU v7x, 256 devices: a whole 4x4x8 slice. The times are simulated.
256 devices in a mesh: cfg: 2 (over core), seq: 16 (over x, z_hi), dp: 8 (over y, z_lo).
Axes of the slice: x: 4, y: 4, z: 8 (z_hi: 4, z_lo: 2; z = z_hi * 2 + z_lo), core: 2. Of those that a mesh axis runs over, the one named last changes fastest.
Arguments:
- image_projections: bfloat16 [2, 16, 2048, 6144], P('cfg', 'dp', 'seq'), may hold values from -8 to 8
- text_projections: bfloat16 [2, 16, 512, 4096], P('cfg', 'dp', 'seq'), may hold values from -6 to 6
- output_weight: bfloat16 [2048, 3072], P('seq', 'dp'), may hold values from -0.125 to 0.125
- image_state: bfloat16 [2, 16, 2048, 3072], P('cfg', 'dp', 'seq'), may hold values from -6 to 6
- modulation: bfloat16 [2, 16, 3, 3072], P('cfg', 'dp'), may hold values from -4 to 4
- final_weight: bfloat16 [3072, 64], replicated, may hold values from -0.109375 to 0.109375
- latent: float32 [16, 2048, 64], P('dp', 'seq'), may hold values from -6 to 6
- next_latent: float32 [16, 2048, 64], P('dp', 'seq'), may hold values from -8 to 8
- timestep: float32 [16], P('dp'), may hold values from 0.3 to 0.8
- rewards: float32 [16], P('dp'), may hold values from -5 to 5
- group_index: int32 [16], P('dp'), may hold values from 0 to 7, as said below
Outputs:
- grad_final_weight: float32 [3072, 64], P('dp')
- log_prob: float32 [16], P('dp')
Inputs may be any that keep to these rules, and one draw needn't show every extreme that they name: `group_index`: each of the 8 prompts has exactly 2 rollouts; rollout 0 shares its prompt with one of the last 2 rollouts.
All inputs are finite; a program needn't handle non-finite values.
Results may differ from a plain program's by a relative error of at most 0.00053.
Values may be sent and summed in bfloat16 or wider, within the bound.
No kernel may reach another device: no remote copies, remote signals or barrier semaphores. Data moves between devices by JAX's collectives and lax.ppermute only.
A program may use at most 64 MiB of HBM per device.

v0:
```python
import functools
import math

import jax
import jax.numpy as jnp
from jax import lax
from jax.experimental import pallas as pl
from jax.experimental.pallas import tpu as pltpu
from jax.sharding import PartitionSpec as P

C = 64
HD = 128
GROUP_SIZE = 2

cfg_scale = 4.5
noise_level = 0.7
step_width = 0.02
norm_eps = 1e-06

X, ZH, Y, ZL = 4, 4, 4, 2
VMEM_BYTES = 32 * 1024 * 1024
HIDDEN_VMEM_BYTES = 50 * 1024 * 1024
FULL_VMEM_BYTES = 61 * 1024 * 1024


def from_x(value, d):
    pairs = [(((x + d) % X) * ZH + z, x * ZH + z) for x in range(X) for z in range(ZH)]
    return lax.ppermute(value, "seq", pairs)


def from_column(value, d):
    def at(core, x, z, y, zl):
        return ((core * X + x) * ZH + z) * (Y * ZL) + y * ZL + zl

    pairs = [
        (at(core if zl == core else 1 - core, x, (z + d) % ZH, y, core), at(core, x, z, y, zl))
        for core in range(2)
        for x in range(X)
        for z in range(ZH)
        for y in range(Y)
        for zl in range(ZL)
    ]
    return lax.ppermute(value, ("cfg", "seq", "dp"), pairs)


def from_zh(value, d):
    pairs = [(x * ZH + (z + d) % ZH, x * ZH + z) for x in range(X) for z in range(ZH)]
    return lax.ppermute(value, "seq", pairs)


def from_y(value, d):
    pairs = [(((y + d) % Y) * ZL + z, y * ZL + z) for y in range(Y) for z in range(ZL)]
    return lax.ppermute(value, "dp", pairs)


def from_zl(value):
    pairs = [(y * ZL + 1 - z, y * ZL + z) for y in range(Y) for z in range(ZL)]
    return lax.ppermute(value, "dp", pairs)


def from_cfg(value):
    return lax.ppermute(value, "cfg", [(0, 1), (1, 0)])


def after(value, *others):
    return lax.optimization_barrier((value,) + others)[0]


def ring_sum(value, fetch):
    first, second, third = (fetch(value, d) for d in (1, 2, 3))
    return (value + second) + (first + third)


def pack_kernel(k_ref, v_ref, kt_ref, vt_ref, q_ref, out_ref):
    rows, text = k_ref.shape[2], kt_ref.shape[2]
    for h in range(out_ref.shape[0]):
        cols = slice(h * HD, (h + 1) * HD)
        at = 0
        for r in range(k_ref.shape[1]):
            for ref, count in ((k_ref, rows), (kt_ref, text), (v_ref, rows), (vt_ref, text)):
                out_ref[h, at : at + count, :] = ref[0, r, :, cols]
                at += count
        out_ref[h, at : at + rows, :] = q_ref[0, 0, :, cols]


def pack_queries_kernel(q_ref, out_ref):
    for h in range(out_ref.shape[0]):
        out_ref[h] = q_ref[0, 0, :, h * HD : (h + 1) * HD]


def pack(image_projections, text_projections):
    _, per_dev, rows, width = image_projections.shape
    text = text_projections.shape[2]
    heads = width // (3 * HD)
    per = 4
    steps = heads // per
    total = per_dev * 2 * (rows + text) + rows

    def spec(rollouts, count, part):
        return pl.BlockSpec((1, rollouts, count, per * HD), lambda h: (0, 0, 0, part * steps + h))

    return pl.pallas_call(
        pack_kernel,
        grid=(steps,),
        in_specs=[
            spec(per_dev, rows, 1),
            spec(per_dev, rows, 2),
            spec(per_dev, text, 0),
            spec(per_dev, text, 1),
            spec(1, rows, 0),
        ],
        out_specs=pl.BlockSpec((per, total, HD), lambda h: (h, 0, 0)),
        out_shape=jax.ShapeDtypeStruct((heads, total, HD), jnp.bfloat16),
        compiler_params=pltpu.CompilerParams(vmem_limit_bytes=FULL_VMEM_BYTES),
        cost_estimate=pl.CostEstimate(
            flops=0, bytes_accessed=2 * heads * total * HD * 2, transcendentals=0
        ),
        name="pack",
    )(image_projections, image_projections, text_projections, text_projections, image_projections)


def pack_queries(image_projections, r):
    _, _, rows, width = image_projections.shape
    heads = width // (3 * HD)
    return pl.pallas_call(
        pack_queries_kernel,
        grid=(1,),
        in_specs=[pl.BlockSpec((1, 1, rows, heads * HD), lambda i: (0, r, 0, 0))],
        out_specs=pl.BlockSpec((heads, rows, HD), lambda i: (0, 0, 0)),
        out_shape=jax.ShapeDtypeStruct((heads, rows, HD), jnp.bfloat16),
        compiler_params=pltpu.CompilerParams(vmem_limit_bytes=VMEM_BYTES),
        cost_estimate=pl.CostEstimate(
            flops=0, bytes_accessed=2 * heads * rows * HD * 2, transcendentals=0
        ),
        name="pack_queries",
    )(image_projections)


def attention_kernel(q_ref, kv_ref, *rest):
    out_ref, keys, values = rest[-3:]
    peers, kv_rows = kv_ref.shape[0], kv_ref.shape[1] // 2
    ones = jnp.ones((kv_rows, HD), jnp.bfloat16)
    for s in range(peers):
        at = slice(s * kv_rows, (s + 1) * kv_rows)
        keys[at, :] = kv_ref[s, 0:kv_rows, :]
        values[at, 0:HD] = kv_ref[s, kv_rows : 2 * kv_rows, :]
        values[at, HD : 2 * HD] = ones

    factor = math.log2(math.e) / math.sqrt(HD)
    for n in range(peers):
        scores = lax.dot_general(
            q_ref[n], keys[...], (((1,), (1,)), ((), ())), preferred_element_type=jnp.float32
        )
        highest = jnp.max(scores, axis=1, keepdims=True)
        powered = jnp.exp2((scores - highest) * factor).astype(jnp.bfloat16)
        sums = jnp.dot(powered, values[...], preferred_element_type=jnp.float32)
        out_ref[n] = (sums[:, 0:HD] / sums[:, HD : HD + 1]).astype(jnp.bfloat16)


def attention(queries, q_at, key_values, r, rows, kv_rows, per_dev, earlier=()):
    peers = queries.shape[0]
    return pl.pallas_call(
        attention_kernel,
        grid=(1,),
        in_specs=[
            pl.BlockSpec((peers, rows, HD), lambda i: (0, q_at, 0)),
            pl.BlockSpec((peers, 2 * kv_rows, HD), lambda i: (0, r, 0)),
        ]
        + [pl.BlockSpec(memory_space=pl.ANY)] * len(earlier),
        out_specs=pl.BlockSpec((peers, rows, HD), lambda i: (0, r, 0)),
        out_shape=jax.ShapeDtypeStruct((peers, per_dev * rows, HD), jnp.bfloat16),
        scratch_shapes=[
            pltpu.VMEM((peers * kv_rows, HD), jnp.bfloat16),
            pltpu.VMEM((peers * kv_rows, 2 * HD), jnp.bfloat16),
        ],
        input_output_aliases={2: 0} if earlier else {},
        compiler_params=pltpu.CompilerParams(vmem_limit_bytes=FULL_VMEM_BYTES),
        cost_estimate=pl.CostEstimate(
            flops=8 * peers * rows * peers * kv_rows * HD,
            bytes_accessed=2 * peers * (2 * rows + 2 * kv_rows) * HD,
            transcendentals=peers * rows * peers * kv_rows,
        ),
        name=f"attention{r}",
    )(queries, key_values, *earlier)


SPANS = ((0, 0), (0, 2), (1, 0), (1, 2), (3, 0), (3, 2), (2, 0), (2, 2))


def hidden_kernel(place, heads_ref, state_any, mods_any, final_any, *rest):
    pieces = rest[: 2 * len(SPANS)]
    hidden_ref, velocity_ref, flat, mixed, weights, state_ref, mods_ref, final_ref, sems = rest[
        2 * len(SPANS) :
    ]
    x_at, zh_at, y_at, c_at = place[0], place[1], place[2], place[3]
    per_dev, rows = state_ref.shape[1], state_ref.shape[2]
    width = weights.shape[2]
    part = weights.shape[1] // X

    def begin(source, target, n):
        copy = pltpu.make_async_copy(source, target, sems.at[n])
        copy.start()
        return copy

    copies = []
    for n, piece in enumerate(pieces):
        core, (turn, first) = n // len(SPANS), SPANS[n % len(SPANS)]
        target = weights.at[core * Y + turn, pl.ds(first * part, piece.shape[0])]
        copies.append(begin(piece, target, n))
        if n == 1:
            mods_copy = begin(mods_any, mods_ref, len(pieces))
            state_copy = begin(state_any, state_ref, len(pieces) + 1)
    final_copy = begin(final_any, final_ref, len(pieces) + 2)
    for i in range(X):
        for j in range(ZH):
            head = lax.rem(x_at + i, X) * ZH + lax.rem(zh_at + j, ZH)
            k = i * ZH + j
            flat[:, k * HD : (k + 1) * HD] = heads_ref[head]
    row_sum = jnp.zeros((per_dev * rows, 1), jnp.float32)
    square_sum = jnp.zeros((per_dev * rows, 1), jnp.float32)
    for core in range(2):
        core_at = c_at if core == 0 else 1 - c_at
        for turn in (0, 1, 3, 2):
            for n, (of_turn, _) in enumerate(SPANS):
                if of_turn == turn:
                    copies[core * len(SPANS) + n].wait()
            at = pl.ds(pl.multiple_of((lax.rem(y_at + turn, Y) * ZL + core_at) * width, 128), width)
            projected = jnp.dot(
                flat[...], weights[core * Y + turn], preferred_element_type=jnp.float32
            )
            if core == 0 and turn == 0:
                mods_copy.wait()
                state_copy.wait()
            for r in range(per_dev):
                gate = mods_ref[0, r : r + 1, at].astype(jnp.float32)
                mixed[r * rows : (r + 1) * rows, at] = (
                    state_ref[0, r, :, at].astype(jnp.float32)
                    + gate * projected[r * rows : (r + 1) * rows]
                )
            block = mixed[:, at]
            row_sum = row_sum + jnp.sum(block, axis=1, keepdims=True)
            square_sum = square_sum + jnp.sum(block * block, axis=1, keepdims=True)
    width_all = mixed.shape[1]
    center = row_sum / width_all
    square = square_sum / width_all
    inverse = lax.rsqrt(square - center * center + norm_eps)
    for r in range(per_dev):
        at = slice(r * rows, (r + 1) * rows)
        scale = 1.0 + mods_ref[2, r : r + 1, :].astype(jnp.float32)
        shift = mods_ref[1, r : r + 1, :].astype(jnp.float32)
        hidden_ref[at, :] = (
            (mixed[at, :] - center[at]) * inverse[at] * scale + shift
        ).astype(jnp.bfloat16)
    final_copy.wait()
    velocity_ref[...] = lax.dot_general(
        final_ref[...], hidden_ref[...], (((1,), (1,)), ((), ())), preferred_element_type=jnp.float32
    )


def hidden_rows(place, heads_part, image_state, modulation, final_weight, pieces):
    heads, all_rows, _ = heads_part.shape
    width_all = image_state.shape[3]
    vmem = pl.BlockSpec(memory_space=pltpu.VMEM)
    return pl.pallas_call(
        hidden_kernel,
        in_specs=[pl.BlockSpec(memory_space=pltpu.SMEM)]
        + [vmem]
        + [pl.BlockSpec(memory_space=pl.ANY)] * (3 + len(pieces)),
        out_specs=[vmem] * 2,
        out_shape=[
            jax.ShapeDtypeStruct((all_rows, width_all), jnp.bfloat16),
            jax.ShapeDtypeStruct((C, all_rows), jnp.float32),
        ],
        scratch_shapes=[
            pltpu.VMEM((all_rows, heads * HD), jnp.bfloat16),
            pltpu.VMEM((all_rows, width_all), jnp.float32),
            pltpu.VMEM((8, heads * HD, pieces[0].shape[1]), jnp.bfloat16),
            pltpu.VMEM(image_state.shape, jnp.bfloat16),
            pltpu.VMEM(modulation.shape, jnp.bfloat16),
            pltpu.VMEM(final_weight.shape, jnp.bfloat16),
            pltpu.SemaphoreType.DMA((len(pieces) + 3,)),
        ],
        compiler_params=pltpu.CompilerParams(vmem_limit_bytes=HIDDEN_VMEM_BYTES),
        cost_estimate=pl.CostEstimate(
            flops=2 * all_rows * heads * HD * width_all,
            bytes_accessed=2 * heads * HD * width_all,
            transcendentals=0,
        ),
        name="hidden",
    )(place, heads_part, image_state, modulation, final_weight, *pieces)


def step_kernel(
    place,
    terms,
    own_ref,
    partner_ref,
    latent_ref,
    next_ref,
    hidden_any,
    keep_ref,
    send_ref,
    squares_ref,
    hidden_ref,
    sem,
):
    copy = pltpu.make_async_copy(hidden_any, hidden_ref, sem)
    copy.start()
    first = place[3] == 0
    own, partner = own_ref[...], partner_ref[...]
    conditional = jnp.where(first, own, partner)
    unconditional = jnp.where(first, partner, own)
    guided = unconditional + cfg_scale * (conditional - unconditional)
    per_dev, _, rows = latent_ref.shape
    row = lax.broadcasted_iota(jnp.int32, squares_ref.shape, 0)
    squares = jnp.zeros(squares_ref.shape, jnp.float32)
    slopes = []
    for r in range(per_dev):
        step_mean = (
            latent_ref[r] * terms[0, r] - guided[:, r * rows : (r + 1) * rows] * terms[1, r]
        )
        residue = next_ref[r] - step_mean
        squares = jnp.where(row == r, jnp.sum(residue * residue), squares)
        slopes.append(terms[2, r] * residue)
    squares_ref[...] = squares
    own_slopes = jnp.where(first, cfg_scale, 1.0 - cfg_scale) * jnp.concatenate(slopes, axis=1)
    half = own_slopes.shape[0] // 2
    low, high = own_slopes[:half], own_slopes[half:]
    ordered = jnp.concatenate([jnp.where(first, low, high), jnp.where(first, high, low)], axis=0)
    copy.wait()
    partial = jnp.dot(
        ordered.astype(jnp.bfloat16), hidden_ref[...], preferred_element_type=jnp.float32
    )
    width = keep_ref.shape[2]
    for n in range(keep_ref.shape[0]):
        cols = slice(n * width, (n + 1) * width)
        keep_ref[n] = partial[:half, cols]
        send_ref[n] = partial[half:, cols]


def step(place, terms, own, partner, latent, next_latent, hidden, data_count):
    rows, width_all = hidden.shape
    cut = (data_count, C // 2, width_all // data_count)
    smem = pl.BlockSpec(memory_space=pltpu.SMEM)
    vmem = pl.BlockSpec(memory_space=pltpu.VMEM)
    return pl.pallas_call(
        step_kernel,
        in_specs=[smem] * 2 + [vmem] * 4 + [pl.BlockSpec(memory_space=pl.ANY)],
        out_specs=[vmem] * 3,
        scratch_shapes=[pltpu.VMEM(hidden.shape, jnp.bfloat16), pltpu.SemaphoreType.DMA],
        out_shape=[
            jax.ShapeDtypeStruct(cut, jnp.float32),
            jax.ShapeDtypeStruct(cut, jnp.float32),
            jax.ShapeDtypeStruct((8, 128), jnp.float32),
        ],
        compiler_params=pltpu.CompilerParams(vmem_limit_bytes=FULL_VMEM_BYTES),
        cost_estimate=pl.CostEstimate(
            flops=2 * rows * C * width_all, bytes_accessed=2 * rows * width_all, transcendentals=0
        ),
        name="step",
    )(place, terms, own, partner, latent, next_latent, hidden)


def fold_kernel(parts_ref, squares_ref, out_ref):
    count, width = parts_ref.shape[1], parts_ref.shape[2]
    out_ref[0:count, :] = jnp.sum(parts_ref[...], axis=0)
    out_ref[count : count + 8, 128:width] = jnp.zeros((8, width - 128), jnp.float32)
    out_ref[count : count + 8, 0:128] = squares_ref[...]


def fold(parts, squares):
    _, count, width = parts.shape
    vmem = pl.BlockSpec(memory_space=pltpu.VMEM)
    return pl.pallas_call(
        fold_kernel,
        in_specs=[vmem] * 2,
        out_specs=vmem,
        out_shape=jax.ShapeDtypeStruct((count + 8, width), jnp.float32),
        name="fold",
    )(parts, squares)


def exchange(send):
    return lax.all_to_all(send, "seq", split_axis=0, concat_axis=0, tiled=True)


def per_device(
    image_projections,
    text_projections,
    output_weight,
    image_state,
    modulation,
    final_weight,
    latent,
    next_latent,
    timestep,
    rewards,
    group_index,
):
    seq_count = lax.axis_size("seq")
    data_count = lax.axis_size("dp")
    per_dev = image_projections.shape[1]
    image_count = image_projections.shape[2]
    width_all = image_state.shape[3]
    rollouts = per_dev * data_count
    seq_at, dp_at, c_at = lax.axis_index("seq"), lax.axis_index("dp"), lax.axis_index("cfg")
    x_at, zh_at, y_at = seq_at // ZH, seq_at % ZH, dp_at // ZL
    place = jnp.stack([x_at, zh_at, y_at, c_at]).astype(jnp.int32)

    kv_rows = image_count + text_projections.shape[2]

    group_count = rollouts // GROUP_SIZE
    member = (group_index[:, None] == jnp.arange(group_count, dtype=jnp.int32)[None, :]).astype(
        jnp.float32
    )
    column = jnp.concatenate([from_column(output_weight, d) for d in range(ZH)], axis=0)
    totals = jnp.sum(member * rewards[:, None], axis=0)
    totals = totals + from_zl(totals)
    first_part = exchange(after(pack(image_projections, text_projections), column, totals))
    totals = ring_sum(totals, from_y)
    advantage = rewards - jnp.sum(member * totals[None, :], axis=1) / GROUP_SIZE
    column = after(column, totals)
    x_parts = [from_x(column, d) for d in range(1, X)]
    first_half = jnp.concatenate([column, x_parts[0]], axis=0)
    second_half = jnp.concatenate(x_parts[1:], axis=0)
    ahead_first, behind_second = from_y(first_half, 1), from_y(second_half, -1)
    ahead_second, behind_first = from_y(second_half, 1), from_y(first_half, -1)
    plane_other = [from_cfg(first_half), from_cfg(second_half)]
    second_part = exchange(
        after(
            pack_queries(image_projections, 1),
            first_part,
            ahead_first,
            behind_second,
            *plane_other,
        )
    )
    far_first, far_second = from_y(ahead_first, 1), from_y(behind_second, -1)
    moved = [ahead_first, ahead_second, behind_first, behind_second, far_first, far_second]
    pieces = [first_half, second_half] + moved + plane_other + [from_cfg(piece) for piece in moved]

    queries_at = per_dev * 2 * kv_rows // image_count
    first_part = after(first_part, ahead_second, behind_first)
    attended = attention(first_part, queries_at, first_part, 0, image_count, kv_rows, per_dev)
    attended = attention(
        second_part, 0, first_part, 1, image_count, kv_rows, per_dev, (attended,)
    )
    spread = noise_level * jnp.sqrt(timestep / (1.0 - timestep))
    drift_gain = 1.0 + spread * spread * (1.0 - timestep) / (2.0 * timestep)
    deviation = spread * math.sqrt(step_width)
    terms = jnp.stack(
        [
            1.0 - spread * spread / (2.0 * timestep) * step_width,
            drift_gain * step_width,
            advantage / (rollouts * C) * drift_gain * step_width / (deviation * deviation),
        ]
    )

    returned = after(exchange(attended), terms)
    hidden, velocity = hidden_rows(
        place, returned, image_state, modulation[0].transpose(1, 0, 2), final_weight.T, pieces
    )
    keep, send, squares = step(
        place,
        terms,
        velocity,
        from_cfg(velocity),
        latent.transpose(0, 2, 1),
        next_latent.transpose(0, 2, 1),
        hidden,
        data_count,
    )

    kept = keep + from_cfg(send)
    share = fold(lax.all_to_all(kept, "dp", split_axis=0, concat_axis=0, tiled=True), squares)
    share = ring_sum(ring_sum(share, from_zh), from_x)
    other = from_cfg(share)
    first = c_at == 0
    half = C // 2
    gradient = jnp.concatenate(
        [jnp.where(first, share, other)[:half], jnp.where(first, other, share)[:half]], axis=0
    ).T
    square_mean = share[half : half + per_dev, 0] / (seq_count * image_count * C)
    log_prob = (
        -square_mean / (2.0 * deviation * deviation)
        - jnp.log(deviation)
        - 0.5 * math.log(2.0 * math.pi)
    )
    return (gradient, log_prob)


def solution(mesh):
    in_specs = (
        P("cfg", "dp", "seq", None),
        P("cfg", "dp", "seq", None),
        P("seq", "dp"),
        P("cfg", "dp", "seq", None),
        P("cfg", "dp", None, None),
        P(),
        P("dp", "seq", None),
        P("dp", "seq", None),
        P("dp"),
        P("dp"),
        P("dp"),
    )
    out_specs = (P("dp", None), P("dp"))
    return jax.shard_map(
        per_device, mesh=mesh, in_specs=in_specs, out_specs=out_specs, check_vma=False
    )
```

profile of v0, /device:TPU:1, one launch (start us, length us, event | category | flops | bytes accessed | tf_op | source)
XLA Modules:
  0.0 244.3 jit_solution(5421700151325706828)
XLA Ops:
  0.6 4.9 %collective-permute-start.4 = (bf16[128,384]{1,0:T(8,128)(2,1)}, bf16[128,384]{1,0:T(8,128)(2,1)S(1)}, u32[]{:S(2)}, u32[]{:S(2)}) collective-permute-start(bf16[128,384]{1,0:T(8,128)(2,1)} %param.13), channel_id=1, source_target_pairs={{0,0},{128,1},{2,2},{130,3},{4,4},{132,5},{6,6},{134,7},{8,8},{136... | collective-permute-start | bytes 294920 | tf_op jit(solution)/shard_map/ppermute | solution.py:43
  5.6 4.5 %collective-permute-start.5 = (bf16[128,384]{1,0:T(8,128)(2,1)}, bf16[128,384]{1,0:T(8,128)(2,1)S(1)}, u32[]{:S(2)}, u32[]{:S(2)}) collective-permute-start(bf16[128,384]{1,0:T(8,128)(2,1)} %param.13), channel_id=1, source_target_pairs={{8,0},{136,1},{10,2},{138,3},{12,4},{140,5},{14,6},{142,7},{16,8},... | collective-permute-start | bytes 294920 | tf_op jit(solution)/shard_map/ppermute | solution.py:43
  10.0 2.2 collective-permute-start.6
  14.4 4.4 %pack.1 = bf16[16,768,128]{2,1,0:T(8,128)(2,1)} custom-call(bf16[1,2,128,6144]{3,2,1,0:T(8,128)(2,1)} %q_ref.3, bf16[1,2,128,6144]{3,2,1,0:T(8,128)(2,1)} %q_ref.3, bf16[1,2,32,4096]{3,2,1,0:T(8,128)(2,1)} %vt_ref.1, bf16[1,2,32,4096]{3,2,1,0:T(8,128)(2,1)} %vt_ref.1, bf16[1,2,128,6144]{3,2,1,0:T(8,128)(2,1)} %q_ref.3), custom_call_target="tpu_custom_call" | custom-call | bytes 6291456 | tf_op jit(solution)/shard_map/pack/pallas_call | solution.py:102
  21.6 7.5 %all-to-all-start = ((bf16[16,768,128]{2,1,0:T(8,128)(2,1)}), bf16[16,768,128]{2,1,0:T(8,128)(2,1)}, u32[]{:S(2)}, u32[]{:S(2)}) async-start(bf16[16,768,128]{2,1,0:T(8,128)(2,1)} %pack.1), calls=%async_computation | async-start | bytes 6291456 | tf_op jit(solution)/shard_map/all_to_all | solution.py:384
  29.1 3.0 %collective-permute-start.1 = (f32[8]{0:T(128)S(1)}, f32[8]{0:T(128)S(1)}, u32[]{:S(2)}, u32[]{:S(2)}) collective-permute-start(f32[8]{0:T(128)S(1)} %add.45), channel_id=1, source_target_pairs={{4,0},{5,1},{6,2},{7,3},{0,4},{1,5},{2,6},{3,7},{12,8},{13,9},{14,... | collective-permute-start | bytes 104 | tf_op jit(solution)/shard_map/ppermute | solution.py:53
  34.5 2.4 collective-permute-done.3
  36.9 2.8 %collective-permute-start.10 = (bf16[512,384]{1,0:T(8,128)(2,1)S(1)}, bf16[512,384]{1,0:T(8,128)(2,1)S(1)}, u32[]{:S(2)}, u32[]{:S(2)}) collective-permute-start(bf16[512,384]{1,0:T(8,128)(2,1)S(1)} %constant_dynamic-update-slice_fusion), channel_id=1, source_target_pairs={{64,0},{72,8},{80,16},{88,24},{96,32},{104,40},{112,48},{120,56},{... | collective-permute-start | bytes 1179656 | tf_op jit(solution)/shard_map/ppermute | solution.py:28
  40.0 2.4 collective-permute-start.8
  42.4 11.2 %collective-permute-done.10 = bf16[512,384]{1,0:T(8,128)(2,1)S(1)} collective-permute-done((bf16[512,384]{1,0:T(8,128)(2,1)S(1)}, bf16[512,384]{1,0:T(8,128)(2,1)S(1)}, u32[]{:S(2)}, u32[]{:S(2)}) %collective-permute-start.10) | collective-permute-done | bytes 393248 | tf_op jit(solution)/shard_map/ppermute | solution.py:28
  53.7 13.6 %collective-permute-done.11 = bf16[512,384]{1,0:T(8,128)(2,1)S(1)} collective-permute-done((bf16[512,384]{1,0:T(8,128)(2,1)S(1)}, bf16[512,384]{1,0:T(8,128)(2,1)S(1)}, u32[]{:S(2)}, u32[]{:S(2)}) %collective-permute-start.11) | collective-permute-done | bytes 393248 | tf_op jit(solution)/shard_map/ppermute | solution.py:28
  72.3 15.1 %collective-permute-done.12.rest_5_ = bf16[1024,384]{1,0:T(8,128)(2,1)S(1)} collective-permute-done((bf16[1024,384]{1,0:T(8,128)(2,1)S(1)}, bf16[1024,384]{1,0:T(8,128)(2,1)S(1)}, u32[]{:S(2)}, u32[]{:S(2)}) %collective-permute-start.12) | collective-permute-done | bytes 786464 | tf_op jit(solution)/shard_map/ppermute | solution.py:53
  90.2 11.6 %all-to-all-done.q_ref.kv_ref = bf16[16,768,128]{2,1,0:T(8,128)(2,1)} async-done(((bf16[16,768,128]{2,1,0:T(8,128)(2,1)}), bf16[16,768,128]{2,1,0:T(8,128)(2,1)}, u32[]{:S(2)}, u32[]{:S(2)}) %all-to-all-start) | async-done | bytes 3145760 | tf_op jit(solution)/shard_map/all_to_all | solution.py:384
  101.8 8.8 %all-to-all-start.1 = ((bf16[16,128,128]{2,1,0:T(8,128)(2,1)}), bf16[16,128,128]{2,1,0:T(8,128)(2,1)}, u32[]{:S(2)}, u32[]{:S(2)}) async-start(bf16[16,128,128]{2,1,0:T(8,128)(2,1)} %pack_queries.1), calls=%async_computation.1 | async-start | bytes 1048576 | tf_op jit(solution)/shard_map/all_to_all | solution.py:384
  110.6 9.2 %attention0.1.rest_0_ = bf16[16,256,128]{2,1,0:T(8,128)(2,1)} custom-call(bf16[16,768,128]{2,1,0:T(8,128)(2,1)} %all-to-all-done.q_ref.kv_ref, bf16[16,768,128]{2,1,0:T(8,128)(2,1)} %all-to-all-done.q_ref.kv_ref), custom_call_target="tpu_custom_call" | custom-call | flops 5368709120 | bytes 2359296 | tf_op jit(solution)/shard_map/attention0/pallas_call | solution.py:162
  119.8 7.8 %all-to-all-done.1.q_ref = bf16[16,128,128]{2,1,0:T(8,128)(2,1)} async-done(((bf16[16,128,128]{2,1,0:T(8,128)(2,1)}), bf16[16,128,128]{2,1,0:T(8,128)(2,1)}, u32[]{:S(2)}, u32[]{:S(2)}) %all-to-all-start.1) | async-done | bytes 524320 | tf_op jit(solution)/shard_map/all_to_all | solution.py:384
  127.6 23.5 %attention1.1 = bf16[16,256,128]{2,1,0:T(8,128)(2,1)} custom-call(bf16[16,128,128]{2,1,0:T(8,128)(2,1)} %all-to-all-done.1.q_ref, bf16[16,768,128]{2,1,0:T(8,128)(2,1)} %all-to-all-done.q_ref.kv_ref, bf16[16,256,128]{2,1,0:T(8,128)(2,1)} %attention0.1.rest_0_), custom_call_target="tpu_custom_call", output_to_operand_aliasing={{}: (2, {})} | custom-call | flops 5368709120 | bytes 2359296 | tf_op jit(solution)/shard_map/attention1/pallas_call | solution.py:162
  151.1 4.3 %all-to-all-start.2 = ((bf16[16,256,128]{2,1,0:T(8,128)(2,1)}), bf16[16,256,128]{2,1,0:T(8,128)(2,1)}, u32[]{:S(2)}, u32[]{:S(2)}) async-start(bf16[16,256,128]{2,1,0:T(8,128)(2,1)} %attention1.1), calls=%async_computation.2 | async-start | bytes 2097152 | tf_op jit(solution)/shard_map/all_to_all | solution.py:384
  156.3 1.9 collective-permute-start.17
  158.2 3.3 %collective-permute-start.22 = (bf16[1024,384]{1,0:T(8,128)(2,1)}, bf16[1024,384]{1,0:T(8,128)(2,1)}, u32[]{:S(2)}, u32[]{:S(2)}) collective-permute-start(bf16[1024,384]{1,0:T(8,128)(2,1)} %copy-done.5), channel_id=1, source_target_pairs={{0,128},{128,0},{1,129},{129,1},{2,130},{130,2},{3,131},{131,3},{4... | collective-permute-start | bytes 2359304 | tf_op jit(solution)/shard_map/ppermute | solution.py:62
  162.1 11.2 %collective-permute-done.18.rest_7_ = bf16[1024,384]{1,0:T(8,128)(2,1)} collective-permute-done((bf16[1024,384]{1,0:T(8,128)(2,1)}, bf16[1024,384]{1,0:T(8,128)(2,1)}, u32[]{:S(2)}, u32[]{:S(2)}) %collective-permute-start.18) | collective-permute-done | bytes 786464 | tf_op jit(solution)/shard_map/ppermute | solution.py:53
  173.3 3.7 %collective-permute-start.21 = (bf16[1024,384]{1,0:T(8,128)(2,1)}, bf16[1024,384]{1,0:T(8,128)(2,1)}, u32[]{:S(2)}, u32[]{:S(2)}) collective-permute-start(bf16[1024,384]{1,0:T(8,128)(2,1)} %collective-permute-done.16.rest_4_), channel_id=1, source_target_pairs={{0,128},{128,0},{1,129},{129,1},{2,130},{130,2},{3,131},{131,3},{4... | collective-permute-start | bytes 2359304 | tf_op jit(solution)/shard_map/ppermute | solution.py:62
  181.5 10.8 %hidden.1 = (bf16[256,3072]{1,0:T(8,128)(2,1)}, f32[64,256]{1,0:T(8,128)S(1)}) custom-call(s32[4]{0:T(128)S(1)} %pad_add_fusion.place, bf16[16,256,128]{2,1,0:T(8,128)(2,1)} %all-to-all-done.2.heads_ref, bf16[1,2,128,3072]{3,2,1,0:T(8,128)(2,1)} %state_any.1, bf16[3,2,3072]{2,1,0:T(2,128)(2,1)S(1)} %bitcast.19, bf16[64,3072]{1,0:T(8,128)(2,1)S(1)} %bitcast.18, ...), custom_call_target="tpu_custom_call" | custom-call | flops 3221225472 | bytes 12582912 | tf_op jit(solution)/shard_map/hidden/pallas_call | solution.py:264
  194.3 3.6 %step.1 = (f32[8,32,384]{2,1,0:T(8,128)}, f32[8,32,384]{2,1,0:T(8,128)}, f32[8,128]{1,0:T(8,128)}) custom-call(s32[4]{0:T(128)} %copy-done.4, f32[3,2]{1,0:T(4,128)} %pad_maximum_fusion.terms, f32[64,256]{1,0:T(8,128)} %copy-done.2, f32[64,256]{1,0:T(8,128)} %copy-done.7, f32[2,64,128]{2,1,0:T(8,128)} %bitcast.20, f32[2,64,128]{2,1,0:T(8,128)} %bitcast.21, ...), custom_call_target="tpu_custom_call" | custom-call | flops 100663296 | bytes 1572864 | tf_op jit(solution)/shard_map/step/pallas_call | solution.py:346
  201.0 17.2 %all_to_all.20.parts_ref = f32[8,32,384]{2,1,0:T(8,128)} all-to-all(f32[8,32,384]{2,1,0:T(8,128)S(1)} %add.49), channel_id=1, replica_groups=mesh['cfg'=2,'seq'=16,'dp'=8] {'dp'}, dimensions={0} | all-to-all | bytes 786432 | tf_op jit(solution)/shard_map/all_to_all | solution.py:475
  219.9 2.7 %collective-permute-start.27 = (f32[40,384]{1,0:T(8,128)}, f32[40,384]{1,0:T(8,128)S(1)}, u32[]{:S(2)}, u32[]{:S(2)}) collective-permute-start(f32[40,384]{1,0:T(8,128)} %fold.1), channel_id=1, source_target_pairs={{16,0},{24,8},{0,16},{8,24},{48,32},{56,40},{32,48},{40,56},{80,64... | collective-permute-start | bytes 184328 | tf_op jit(solution)/shard_map/ppermute | solution.py:48
  222.9 2.1 collective-permute-start.29
  225.0 2.1 collective-permute-done.27
  227.1 2.0 collective-permute-done.28
  230.0 3.1 %collective-permute-start.30 = (f32[40,384]{1,0:T(8,128)S(1)}, f32[40,384]{1,0:T(8,128)S(1)}, u32[]{:S(2)}, u32[]{:S(2)}) collective-permute-start(f32[40,384]{1,0:T(8,128)S(1)} %add_add_fusion.1), channel_id=1, source_target_pairs={{64,0},{72,8},{80,16},{88,24},{96,32},{104,40},{112,48},{120,56},{... | collective-permute-start | bytes 184328 | tf_op jit(solution)/shard_map/ppermute | solution.py:28
  236.2 1.9 collective-permute-done.32
  238.1 4.5 %collective-permute-start.33 = (f32[40,384]{1,0:T(8,128)S(1)}, f32[40,384]{1,0:T(8,128)S(1)}, u32[]{:S(2)}, u32[]{:S(2)}) collective-permute-start(f32[40,384]{1,0:T(8,128)S(1)} %add_add_fusion), channel_id=1, source_target_pairs={{0,128},{128,0},{1,129},{129,1},{2,130},{130,2},{3,131},{131,3},{4... | collective-permute-start | bytes 184328 | tf_op jit(solution)/shard_map/ppermute | solution.py:62
  (96 shorter events, 34.0 us)
Async XLA Ops:
  0.6 18.2 %collective-permute-start.4 = (bf16[128,384]{1,0:T(8,128)(2,1)}, bf16[128,384]{1,0:T(8,128)(2,1)S(1)}, u32[]{:S(2)}, u32[]{:S(2)}) collective-permute-start(bf16[128,384]{1,0:T(8,128)(2,1)} %param.13), channel_id=1, source_target_pairs={{0,0},{128,1},{2,2},{130,3},{4,4},{132,5},{6,6},{134,7},{8,8},{136... | collective-permute-start | bytes 294920 | tf_op jit(solution)/shard_map/ppermute | solution.py:43
  5.6 13.3 %collective-permute-start.5 = (bf16[128,384]{1,0:T(8,128)(2,1)}, bf16[128,384]{1,0:T(8,128)(2,1)S(1)}, u32[]{:S(2)}, u32[]{:S(2)}) collective-permute-start(bf16[128,384]{1,0:T(8,128)(2,1)} %param.13), channel_id=1, source_target_pairs={{8,0},{136,1},{10,2},{138,3},{12,4},{140,5},{14,6},{142,7},{16,8},... | collective-permute-start | bytes 294920 | tf_op jit(solution)/shard_map/ppermute | solution.py:43
  10.0 10.1 %collective-permute-start.6 = (bf16[128,384]{1,0:T(8,128)(2,1)}, bf16[128,384]{1,0:T(8,128)(2,1)S(1)}, u32[]{:S(2)}, u32[]{:S(2)}) collective-permute-start(bf16[128,384]{1,0:T(8,128)(2,1)} %param.13), channel_id=1, source_target_pairs={{16,0},{144,1},{18,2},{146,3},{20,4},{148,5},{22,6},{150,7},{24,8}... | collective-permute-start | bytes 294920 | tf_op jit(solution)/shard_map/ppermute | solution.py:43
  12.2 9.4 %collective-permute-start.7 = (bf16[128,384]{1,0:T(8,128)(2,1)}, bf16[128,384]{1,0:T(8,128)(2,1)S(1)}, u32[]{:S(2)}, u32[]{:S(2)}) collective-permute-start(bf16[128,384]{1,0:T(8,128)(2,1)} %param.13), channel_id=1, source_target_pairs={{24,0},{152,1},{26,2},{154,3},{28,4},{156,5},{30,6},{158,7},{0,8},... | collective-permute-start | bytes 294920 | tf_op jit(solution)/shard_map/ppermute | solution.py:43
  14.3 4.5 %collective-permute-start = (f32[8]{0:T(128)S(1)}, f32[8]{0:T(128)S(1)}, u32[]{:S(2)}, u32[]{:S(2)}) collective-permute-start(f32[8]{0:T(128)S(1)} %select_reduce_fusion.1), channel_id=1, source_target_pairs={{1,0},{0,1},{3,2},{2,3},{5,4},{4,5},{7,6},{6,7},{9,8},{8,9},{11,10... | collective-permute-start | bytes 104 | tf_op jit(solution)/shard_map/ppermute | solution.py:58
  21.6 80.1 %all-to-all-start = ((bf16[16,768,128]{2,1,0:T(8,128)(2,1)}), bf16[16,768,128]{2,1,0:T(8,128)(2,1)}, u32[]{:S(2)}, u32[]{:S(2)}) async-start(bf16[16,768,128]{2,1,0:T(8,128)(2,1)} %pack.1), calls=%async_computation | async-start | bytes 6291456 | tf_op jit(solution)/shard_map/all_to_all | solution.py:384
  29.1 4.4 %collective-permute-start.1 = (f32[8]{0:T(128)S(1)}, f32[8]{0:T(128)S(1)}, u32[]{:S(2)}, u32[]{:S(2)}) collective-permute-start(f32[8]{0:T(128)S(1)} %add.45), channel_id=1, source_target_pairs={{4,0},{5,1},{6,2},{7,3},{0,4},{1,5},{2,6},{3,7},{12,8},{13,9},{14,... | collective-permute-start | bytes 104 | tf_op jit(solution)/shard_map/ppermute | solution.py:53
  32.9 4.0 %collective-permute-start.3 = (f32[8]{0:T(128)S(1)}, f32[8]{0:T(128)S(1)}, u32[]{:S(2)}, u32[]{:S(2)}) collective-permute-start(f32[8]{0:T(128)S(1)} %add.45), channel_id=1, source_target_pairs={{6,0},{7,1},{0,2},{1,3},{2,4},{3,5},{4,6},{5,7},{14,8},{15,9},{8,1... | collective-permute-start | bytes 104 | tf_op jit(solution)/shard_map/ppermute | solution.py:53
  36.9 16.7 %collective-permute-start.10 = (bf16[512,384]{1,0:T(8,128)(2,1)S(1)}, bf16[512,384]{1,0:T(8,128)(2,1)S(1)}, u32[]{:S(2)}, u32[]{:S(2)}) collective-permute-start(bf16[512,384]{1,0:T(8,128)(2,1)S(1)} %constant_dynamic-update-slice_fusion), channel_id=1, source_target_pairs={{64,0},{72,8},{80,16},{88,24},{96,32},{104,40},{112,48},{120,56},{... | collective-permute-start | bytes 1179656 | tf_op jit(solution)/shard_map/ppermute | solution.py:28
  39.7 27.5 %collective-permute-start.11 = (bf16[512,384]{1,0:T(8,128)(2,1)S(1)}, bf16[512,384]{1,0:T(8,128)(2,1)S(1)}, u32[]{:S(2)}, u32[]{:S(2)}) collective-permute-start(bf16[512,384]{1,0:T(8,128)(2,1)S(1)} %constant_dynamic-update-slice_fusion), channel_id=1, source_target_pairs={{96,0},{104,8},{112,16},{120,24},{0,32},{8,40},{16,48},{24,56},{32... | collective-permute-start | bytes 1179656 | tf_op jit(solution)/shard_map/ppermute | solution.py:28
  40.0 28.7 %collective-permute-start.8 = (bf16[512,384]{1,0:T(8,128)(2,1)S(1)}, bf16[512,384]{1,0:T(8,128)(2,1)S(1)}, u32[]{:S(2)}, u32[]{:S(2)}) collective-permute-start(bf16[512,384]{1,0:T(8,128)(2,1)S(1)} %constant_dynamic-update-slice_fusion), channel_id=1, source_target_pairs={{32,0},{40,8},{48,16},{56,24},{64,32},{72,40},{80,48},{88,56},{96,... | collective-permute-start | bytes 1179656 | tf_op jit(solution)/shard_map/ppermute | solution.py:28
  67.3 20.1 %collective-permute-start.12 = (bf16[1024,384]{1,0:T(8,128)(2,1)S(1)}, bf16[1024,384]{1,0:T(8,128)(2,1)S(1)}, u32[]{:S(2)}, u32[]{:S(2)}) collective-permute-start(bf16[1024,384]{1,0:T(8,128)(2,1)S(1)} %constant_dynamic-update-slice_fusion.6.rest_1_), channel_id=1, source_target_pairs={{6,0},{7,1},{0,2},{1,3},{2,4},{3,5},{4,6},{5,7},{14,8},{15,9},{8,1... | collective-permute-start | bytes 2359304 | tf_op jit(solution)/shard_map/ppermute | solution.py:53
  68.8 20.5 %collective-permute-start.9 = (bf16[1024,384]{1,0:T(8,128)(2,1)S(1)}, bf16[1024,384]{1,0:T(8,128)(2,1)S(1)}, u32[]{:S(2)}, u32[]{:S(2)}) collective-permute-start(bf16[1024,384]{1,0:T(8,128)(2,1)S(1)} %constant_dynamic-update-slice_fusion.4.rest_0_), channel_id=1, source_target_pairs={{2,0},{3,1},{4,2},{5,3},{6,4},{7,5},{0,6},{1,7},{10,8},{11,9},{12,... | collective-permute-start | bytes 2359304 | tf_op jit(solution)/shard_map/ppermute | solution.py:53
  70.3 19.0 %collective-permute-start.14 = (bf16[1024,384]{1,0:T(8,128)(2,1)S(1)}, bf16[1024,384]{1,0:T(8,128)(2,1)S(1)}, u32[]{:S(2)}, u32[]{:S(2)}) collective-permute-start(bf16[1024,384]{1,0:T(8,128)(2,1)S(1)} %constant_dynamic-update-slice_fusion.6.rest_1_), channel_id=1, source_target_pairs={{0,128},{128,0},{1,129},{129,1},{2,130},{130,2},{3,131},{131,3},{4... | collective-permute-start | bytes 2359304 | tf_op jit(solution)/shard_map/ppermute | solution.py:62
  71.3 18.9 %collective-permute-start.13 = (bf16[1024,384]{1,0:T(8,128)(2,1)S(1)}, bf16[1024,384]{1,0:T(8,128)(2,1)}, u32[]{:S(2)}, u32[]{:S(2)}) collective-permute-start(bf16[1024,384]{1,0:T(8,128)(2,1)S(1)} %constant_dynamic-update-slice_fusion.4.rest_0_), channel_id=1, source_target_pairs={{0,128},{128,0},{1,129},{129,1},{2,130},{130,2},{3,131},{131,3},{4... | collective-permute-start | bytes 2359304 | tf_op jit(solution)/shard_map/ppermute | solution.py:62
  71.3 39.3 %collective-permute-start.15 = (bf16[1024,384]{1,0:T(8,128)(2,1)S(1)}, bf16[1024,384]{1,0:T(8,128)(2,1)}, u32[]{:S(2)}, u32[]{:S(2)}) collective-permute-start(bf16[1024,384]{1,0:T(8,128)(2,1)S(1)} %constant_dynamic-update-slice_fusion.6.rest_1_), channel_id=1, source_target_pairs={{2,0},{3,1},{4,2},{5,3},{6,4},{7,5},{0,6},{1,7},{10,8},{11,9},{12,... | collective-permute-start | bytes 2359304 | tf_op jit(solution)/shard_map/ppermute | solution.py:53
  88.3 22.3 %collective-permute-start.16 = (bf16[1024,384]{1,0:T(8,128)(2,1)S(1)}, bf16[1024,384]{1,0:T(8,128)(2,1)}, u32[]{:S(2)}, u32[]{:S(2)}) collective-permute-start(bf16[1024,384]{1,0:T(8,128)(2,1)S(1)} %constant_dynamic-update-slice_fusion.4.rest_0_), channel_id=1, source_target_pairs={{6,0},{7,1},{0,2},{1,3},{2,4},{3,5},{4,6},{5,7},{14,8},{15,9},{8,1... | collective-permute-start | bytes 2359304 | tf_op jit(solution)/shard_map/ppermute | solution.py:53
  101.8 25.9 %all-to-all-start.1 = ((bf16[16,128,128]{2,1,0:T(8,128)(2,1)}), bf16[16,128,128]{2,1,0:T(8,128)(2,1)}, u32[]{:S(2)}, u32[]{:S(2)}) async-start(bf16[16,128,128]{2,1,0:T(8,128)(2,1)} %pack_queries.1), calls=%async_computation.1 | async-start | bytes 1048576 | tf_op jit(solution)/shard_map/all_to_all | solution.py:384
  151.1 27.3 %all-to-all-start.2 = ((bf16[16,256,128]{2,1,0:T(8,128)(2,1)}), bf16[16,256,128]{2,1,0:T(8,128)(2,1)}, u32[]{:S(2)}, u32[]{:S(2)}) async-start(bf16[16,256,128]{2,1,0:T(8,128)(2,1)} %attention1.1), calls=%async_computation.2 | async-start | bytes 2097152 | tf_op jit(solution)/shard_map/all_to_all | solution.py:384
  155.4 17.9 %collective-permute-start.18 = (bf16[1024,384]{1,0:T(8,128)(2,1)}, bf16[1024,384]{1,0:T(8,128)(2,1)}, u32[]{:S(2)}, u32[]{:S(2)}) collective-permute-start(bf16[1024,384]{1,0:T(8,128)(2,1)} %copy-done.5), channel_id=1, source_target_pairs={{6,0},{7,1},{0,2},{1,3},{2,4},{3,5},{4,6},{5,7},{14,8},{15,9},{8,1... | collective-permute-start | bytes 2359304 | tf_op jit(solution)/shard_map/ppermute | solution.py:53
  156.3 20.7 %collective-permute-start.17 = (bf16[1024,384]{1,0:T(8,128)(2,1)S(1)}, bf16[1024,384]{1,0:T(8,128)(2,1)}, u32[]{:S(2)}, u32[]{:S(2)}) collective-permute-start(bf16[1024,384]{1,0:T(8,128)(2,1)S(1)} %collective-permute-done.9.rest_2_), channel_id=1, source_target_pairs={{2,0},{3,1},{4,2},{5,3},{6,4},{7,5},{0,6},{1,7},{10,8},{11,9},{12,... | collective-permute-start | bytes 2359304 | tf_op jit(solution)/shard_map/ppermute | solution.py:53
  158.2 18.8 %collective-permute-start.22 = (bf16[1024,384]{1,0:T(8,128)(2,1)}, bf16[1024,384]{1,0:T(8,128)(2,1)}, u32[]{:S(2)}, u32[]{:S(2)}) collective-permute-start(bf16[1024,384]{1,0:T(8,128)(2,1)} %copy-done.5), channel_id=1, source_target_pairs={{0,128},{128,0},{1,129},{129,1},{2,130},{130,2},{3,131},{131,3},{4... | collective-permute-start | bytes 2359304 | tf_op jit(solution)/shard_map/ppermute | solution.py:62
  161.5 16.9 %collective-permute-start.19 = (bf16[1024,384]{1,0:T(8,128)(2,1)S(1)}, bf16[1024,384]{1,0:T(8,128)(2,1)}, u32[]{:S(2)}, u32[]{:S(2)}) collective-permute-start(bf16[1024,384]{1,0:T(8,128)(2,1)S(1)} %collective-permute-done.9.rest_2_), channel_id=1, source_target_pairs={{0,128},{128,0},{1,129},{129,1},{2,130},{130,2},{3,131},{131,3},{4... | collective-permute-start | bytes 2359304 | tf_op jit(solution)/shard_map/ppermute | solution.py:62
  161.6 16.8 %collective-permute-start.20 = (bf16[1024,384]{1,0:T(8,128)(2,1)}, bf16[1024,384]{1,0:T(8,128)(2,1)}, u32[]{:S(2)}, u32[]{:S(2)}) collective-permute-start(bf16[1024,384]{1,0:T(8,128)(2,1)} %collective-permute-done.15.rest_3_), channel_id=1, source_target_pairs={{0,128},{128,0},{1,129},{129,1},{2,130},{130,2},{3,131},{131,3},{4... | collective-permute-start | bytes 2359304 | tf_op jit(solution)/shard_map/ppermute | solution.py:62
  173.3 5.9 %collective-permute-start.21 = (bf16[1024,384]{1,0:T(8,128)(2,1)}, bf16[1024,384]{1,0:T(8,128)(2,1)}, u32[]{:S(2)}, u32[]{:S(2)}) collective-permute-start(bf16[1024,384]{1,0:T(8,128)(2,1)} %collective-permute-done.16.rest_4_), channel_id=1, source_target_pairs={{0,128},{128,0},{1,129},{129,1},{2,130},{130,2},{3,131},{131,3},{4... | collective-permute-start | bytes 2359304 | tf_op jit(solution)/shard_map/ppermute | solution.py:62
  177.0 4.5 %collective-permute-start.23 = (bf16[1024,384]{1,0:T(8,128)(2,1)}, bf16[1024,384]{1,0:T(8,128)(2,1)}, u32[]{:S(2)}, u32[]{:S(2)}) collective-permute-start(bf16[1024,384]{1,0:T(8,128)(2,1)} %collective-permute-done.17.rest_6_), channel_id=1, source_target_pairs={{0,128},{128,0},{1,129},{129,1},{2,130},{130,2},{3,131},{131,3},{4... | collective-permute-start | bytes 2359304 | tf_op jit(solution)/shard_map/ppermute | solution.py:62
  219.9 7.3 %collective-permute-start.27 = (f32[40,384]{1,0:T(8,128)}, f32[40,384]{1,0:T(8,128)S(1)}, u32[]{:S(2)}, u32[]{:S(2)}) collective-permute-start(f32[40,384]{1,0:T(8,128)} %fold.1), channel_id=1, source_target_pairs={{16,0},{24,8},{0,16},{8,24},{48,32},{56,40},{32,48},{40,56},{80,64... | collective-permute-start | bytes 184328 | tf_op jit(solution)/shard_map/ppermute | solution.py:48
  222.6 6.5 %collective-permute-start.28 = (f32[40,384]{1,0:T(8,128)}, f32[40,384]{1,0:T(8,128)S(1)}, u32[]{:S(2)}, u32[]{:S(2)}) collective-permute-start(f32[40,384]{1,0:T(8,128)} %fold.1), channel_id=1, source_target_pairs={{8,0},{16,8},{24,16},{0,24},{40,32},{48,40},{56,48},{32,56},{72,64... | collective-permute-start | bytes 184328 | tf_op jit(solution)/shard_map/ppermute | solution.py:48
  222.9 6.2 %collective-permute-start.29 = (f32[40,384]{1,0:T(8,128)}, f32[40,384]{1,0:T(8,128)S(1)}, u32[]{:S(2)}, u32[]{:S(2)}) collective-permute-start(f32[40,384]{1,0:T(8,128)} %fold.1), channel_id=1, source_target_pairs={{24,0},{0,8},{8,16},{16,24},{56,32},{32,40},{40,48},{48,56},{88,64... | collective-permute-start | bytes 184328 | tf_op jit(solution)/shard_map/ppermute | solution.py:48
  230.0 4.8 %collective-permute-start.30 = (f32[40,384]{1,0:T(8,128)S(1)}, f32[40,384]{1,0:T(8,128)S(1)}, u32[]{:S(2)}, u32[]{:S(2)}) collective-permute-start(f32[40,384]{1,0:T(8,128)S(1)} %add_add_fusion.1), channel_id=1, source_target_pairs={{64,0},{72,8},{80,16},{88,24},{96,32},{104,40},{112,48},{120,56},{... | collective-permute-start | bytes 184328 | tf_op jit(solution)/shard_map/ppermute | solution.py:28
  233.8 4.3 %collective-permute-start.32 = (f32[40,384]{1,0:T(8,128)S(1)}, f32[40,384]{1,0:T(8,128)S(1)}, u32[]{:S(2)}, u32[]{:S(2)}) collective-permute-start(f32[40,384]{1,0:T(8,128)S(1)} %add_add_fusion.1), channel_id=1, source_target_pairs={{96,0},{104,8},{112,16},{120,24},{0,32},{8,40},{16,48},{24,56},{32... | collective-permute-start | bytes 184328 | tf_op jit(solution)/shard_map/ppermute | solution.py:28
  238.1 5.4 %collective-permute-start.33 = (f32[40,384]{1,0:T(8,128)S(1)}, f32[40,384]{1,0:T(8,128)S(1)}, u32[]{:S(2)}, u32[]{:S(2)}) collective-permute-start(f32[40,384]{1,0:T(8,128)S(1)} %add_add_fusion), channel_id=1, source_target_pairs={{0,128},{128,0},{1,129},{129,1},{2,130},{130,2},{3,131},{131,3},{4... | collective-permute-start | bytes 184328 | tf_op jit(solution)/shard_map/ppermute | solution.py:62
  (16 other events, 370.8 us)
where the time goes:
time: 247 us; the launch traced here: 244 us
  waiting for transfers between devices  89.9 us (36%)
  starting transfers between devices  74.5 us (30%)
  Pallas kernels  54.1 us (22%)
  blocking collectives  17.2 us (7%)
  other arithmetic  4.87 us (2%)
  local copies, waits for them, and re-layouts  2.7 us (1%)
    pallas_call x2, Pallas kernels, attention(): pl.pallas_call(attention_kernel, grid=(1,), in_specs=[pl.BlockSpec((peers...  32.6 us
    ppermute x9, waiting for transfers between devices, from_y(): return lax.ppermute(value, 'dp', pairs)  29.6 us
    ppermute x6, waiting for transfers between devices, from_x(): return lax.ppermute(value, 'seq', pairs)  28.3 us
    all_to_all x3, starting transfers between devices, exchange(): return lax.all_to_all(send, 'seq', split_axis=0, concat_axis=0, tiled=True)  20.7 us
    all_to_all x3, waiting for transfers between devices, exchange(): return lax.all_to_all(send, 'seq', split_axis=0, concat_axis=0, tiled=True)  19.4 us
    all_to_all x1, blocking collectives, per_device(): lax.all_to_all(kept, 'dp', split_axis=0, concat_axis=0, tiled=True)  17.2 us
    ppermute x11, starting transfers between devices, from_cfg(): return lax.ppermute(value, 'cfg', [(0, 1), (1, 0)])  14.4 us
    ppermute x4, starting transfers between devices, from_column(): return lax.ppermute(value, ('cfg', 'seq', 'dp'), pairs)  12.9 us
  transfers between devices with their start and end apart: 37, of which 21 were waited for; matrix products, arithmetic and copies ran while one was open for 1% of the time, Pallas kernels for 6%

commit v1 on v0

--- a/solution.py
+++ b/solution.py
@@ -20,6 +20,7 @@
 X, ZH, Y, ZL = 4, 4, 4, 2
 VMEM_BYTES = 32 * 1024 * 1024
 HIDDEN_VMEM_BYTES = 50 * 1024 * 1024
+ATTENTION_STEPS = 4
 FULL_VMEM_BYTES = 61 * 1024 * 1024
 
 
@@ -73,19 +74,26 @@
 
 def pack_kernel(k_ref, v_ref, kt_ref, vt_ref, q_ref, out_ref):
     rows, text = k_ref.shape[2], kt_ref.shape[2]
-    for h in range(out_ref.shape[0]):
-        cols = slice(h * HD, (h + 1) * HD)
+
+    def pack_head(h, carry):
+        cols = pl.ds(pl.multiple_of(h * HD, HD), HD)
         at = 0
         for r in range(k_ref.shape[1]):
             for ref, count in ((k_ref, rows), (kt_ref, text), (v_ref, rows), (vt_ref, text)):
                 out_ref[h, at : at + count, :] = ref[0, r, :, cols]
                 at += count
         out_ref[h, at : at + rows, :] = q_ref[0, 0, :, cols]
+        return carry
+
+    lax.fori_loop(0, out_ref.shape[0], pack_head, 0)
 
 
 def pack_queries_kernel(q_ref, out_ref):
-    for h in range(out_ref.shape[0]):
-        out_ref[h] = q_ref[0, 0, :, h * HD : (h + 1) * HD]
+    def pack_head(h, carry):
+        out_ref[h] = q_ref[0, 0, :, pl.ds(pl.multiple_of(h * HD, HD), HD)]
+        return carry
+
+    lax.fori_loop(0, out_ref.shape[0], pack_head, 0)
 
 
 def pack(image_projections, text_projections):
@@ -139,15 +147,22 @@
 def attention_kernel(q_ref, kv_ref, *rest):
     out_ref, keys, values = rest[-3:]
     peers, kv_rows = kv_ref.shape[0], kv_ref.shape[1] // 2
-    ones = jnp.ones((kv_rows, HD), jnp.bfloat16)
-    for s in range(peers):
-        at = slice(s * kv_rows, (s + 1) * kv_rows)
-        keys[at, :] = kv_ref[s, 0:kv_rows, :]
-        values[at, 0:HD] = kv_ref[s, kv_rows : 2 * kv_rows, :]
-        values[at, HD : 2 * HD] = ones
+
+    @pl.when(pl.program_id(0) == 0)
+    def _():
+        ones = jnp.ones((kv_rows, HD), jnp.bfloat16)
+
+        def place_peer(s, carry):
+            at = pl.ds(pl.multiple_of(s * kv_rows, kv_rows), kv_rows)
+            keys[at, :] = kv_ref[s, 0:kv_rows, :]
+            values[at, 0:HD] = kv_ref[s, kv_rows : 2 * kv_rows, :]
+            values[at, HD : 2 * HD] = ones
+            return carry
+
+        lax.fori_loop(0, peers, place_peer, 0)
 
     factor = math.log2(math.e) / math.sqrt(HD)
-    for n in range(peers):
+    for n in range(q_ref.shape[0]):
         scores = lax.dot_general(
             q_ref[n], keys[...], (((1,), (1,)), ((), ())), preferred_element_type=jnp.float32
         )
@@ -161,13 +176,13 @@
     peers = queries.shape[0]
     return pl.pallas_call(
         attention_kernel,
-        grid=(1,),
+        grid=(ATTENTION_STEPS,),
         in_specs=[
-            pl.BlockSpec((peers, rows, HD), lambda i: (0, q_at, 0)),
+            pl.BlockSpec((peers // ATTENTION_STEPS, rows, HD), lambda i: (i, q_at, 0)),
             pl.BlockSpec((peers, 2 * kv_rows, HD), lambda i: (0, r, 0)),
         ]
         + [pl.BlockSpec(memory_space=pl.ANY)] * len(earlier),
-        out_specs=pl.BlockSpec((peers, rows, HD), lambda i: (0, r, 0)),
+        out_specs=pl.BlockSpec((peers // ATTENTION_STEPS, rows, HD), lambda i: (i, r, 0)),
         out_shape=jax.ShapeDtypeStruct((peers, per_dev * rows, HD), jnp.bfloat16),
         scratch_shapes=[
             pltpu.VMEM((peers * kv_rows, HD), jnp.bfloat16),
@@ -297,15 +312,11 @@
     partner_ref,
     latent_ref,
     next_ref,
-    hidden_any,
+    hidden_ref,
     keep_ref,
     send_ref,
     squares_ref,
-    hidden_ref,
-    sem,
 ):
-    copy = pltpu.make_async_copy(hidden_any, hidden_ref, sem)
-    copy.start()
     first = place[3] == 0
     own, partner = own_ref[...], partner_ref[...]
     conditional = jnp.where(first, own, partner)
@@ -327,7 +338,6 @@
     half = own_slopes.shape[0] // 2
     low, high = own_slopes[:half], own_slopes[half:]
     ordered = jnp.concatenate([jnp.where(first, low, high), jnp.where(first, high, low)], axis=0)
-    copy.wait()
     partial = jnp.dot(
         ordered.astype(jnp.bfloat16), hidden_ref[...], preferred_element_type=jnp.float32
     )
@@ -345,15 +355,14 @@
     vmem = pl.BlockSpec(memory_space=pltpu.VMEM)
     return pl.pallas_call(
         step_kernel,
-        in_specs=[smem] * 2 + [vmem] * 4 + [pl.BlockSpec(memory_space=pl.ANY)],
+        in_specs=[smem] * 2 + [vmem] * 5,
         out_specs=[vmem] * 3,
-        scratch_shapes=[pltpu.VMEM(hidden.shape, jnp.bfloat16), pltpu.SemaphoreType.DMA],
         out_shape=[
             jax.ShapeDtypeStruct(cut, jnp.float32),
             jax.ShapeDtypeStruct(cut, jnp.float32),
             jax.ShapeDtypeStruct((8, 128), jnp.float32),
         ],
-        compiler_params=pltpu.CompilerParams(vmem_limit_bytes=FULL_VMEM_BYTES),
+        compiler_params=pltpu.CompilerParams(vmem_limit_bytes=VMEM_BYTES),
         cost_estimate=pl.CostEstimate(
             flops=2 * rows * C * width_all, bytes_accessed=2 * rows * width_all, transcendentals=0
         ),

time: 247 us -> 232 us (0.939)
  Pallas kernels: 54.1 us -> 41.5 us
  starting transfers between devices: 74.5 us -> 78.2 us
    pallas_call x3, Pallas kernels: 36.3 us -> 23.5 us  [the longest x2 22.6 us: attention(): pl.pallas_call(attention_kernel, grid=(ATTENTION_STEPS,), in_specs=[pl.Bl...]
  transfers between devices with their start and end apart: 37 -> 37, of which waited for: 21 -> 22; matrix products, arithmetic and copies ran while one was open for 1% -> 1% of each run, Pallas kernels for 6% -> 7%
where the time goes in v1:
time: 232 us; the launch traced here: 231 us
  waiting for transfers between devices  88.4 us (38%)
  starting transfers between devices  78.2 us (34%)
  Pallas kernels  41.5 us (18%)
  blocking collectives  15.5 us (7%)
  local copies, waits for them, and re-layouts  3.5 us (2%)
  other arithmetic  3.28 us (1%)
    ppermute x9, waiting for transfers between devices, from_y(): return lax.ppermute(value, 'dp', pairs)  29.6 us
    ppermute x6, waiting for transfers between devices, from_x(): return lax.ppermute(value, 'seq', pairs)  28.8 us
    pallas_call x2, Pallas kernels, attention(): pl.pallas_call(attention_kernel, grid=(ATTENTION_STEPS,), in_specs=[pl.Bl...  22.6 us
    all_to_all x3, starting transfers between devices, exchange(): return lax.all_to_all(send, 'seq', split_axis=0, concat_axis=0, tiled=True)  22.3 us
    all_to_all x3, waiting for transfers between devices, exchange(): return lax.all_to_all(send, 'seq', split_axis=0, concat_axis=0, tiled=True)  17 us
    all_to_all x1, blocking collectives, per_device(): lax.all_to_all(kept, 'dp', split_axis=0, concat_axis=0, tiled=True)  15.5 us
    ppermute x11, starting transfers between devices, from_cfg(): return lax.ppermute(value, 'cfg', [(0, 1), (1, 0)])  14.6 us
    ppermute x4, starting transfers between devices, from_column(): return lax.ppermute(value, ('cfg', 'seq', 'dp'), pairs)  12.9 us
  transfers between devices with their start and end apart: 37, of which 22 were waited for; matrix products, arithmetic and copies ran while one was open for 1% of the time, Pallas kernels for 7%

profile of v1, /device:TPU:1, one launch (start us, length us, event | category | flops | bytes accessed | tf_op | source)
XLA Modules:
  0.0 231.2 jit_solution(16786908226226811509)
XLA Ops:
  0.6 4.9 %collective-permute-start.4 = (bf16[128,384]{1,0:T(8,128)(2,1)}, bf16[128,384]{1,0:T(8,128)(2,1)S(1)}, u32[]{:S(2)}, u32[]{:S(2)}) collective-permute-start(bf16[128,384]{1,0:T(8,128)(2,1)} %param.13), channel_id=1, source_target_pairs={{0,0},{128,1},{2,2},{130,3},{4,4},{132,5},{6,6},{134,7},{8,8},{136... | collective-permute-start | bytes 294920 | tf_op jit(solution)/shard_map/ppermute | solution.py:44
  5.6 4.5 %collective-permute-start.5 = (bf16[128,384]{1,0:T(8,128)(2,1)}, bf16[128,384]{1,0:T(8,128)(2,1)S(1)}, u32[]{:S(2)}, u32[]{:S(2)}) collective-permute-start(bf16[128,384]{1,0:T(8,128)(2,1)} %param.13), channel_id=1, source_target_pairs={{8,0},{136,1},{10,2},{138,3},{12,4},{140,5},{14,6},{142,7},{16,8},... | collective-permute-start | bytes 294920 | tf_op jit(solution)/shard_map/ppermute | solution.py:44
  10.0 2.2 collective-permute-start.6
  14.4 4.5 %pack.1 = bf16[16,768,128]{2,1,0:T(8,128)(2,1)} custom-call(bf16[1,2,128,6144]{3,2,1,0:T(8,128)(2,1)} %q_ref.3, bf16[1,2,128,6144]{3,2,1,0:T(8,128)(2,1)} %q_ref.3, bf16[1,2,32,4096]{3,2,1,0:T(8,128)(2,1)} %vt_ref.1, bf16[1,2,32,4096]{3,2,1,0:T(8,128)(2,1)} %vt_ref.1, bf16[1,2,128,6144]{3,2,1,0:T(8,128)(2,1)} %q_ref.3), custom_call_target="tpu_custom_call" | custom-call | bytes 6291456 | tf_op jit(solution)/shard_map/pack/pallas_call | solution.py:110
  21.6 7.5 %all-to-all-start = ((bf16[16,768,128]{2,1,0:T(8,128)(2,1)}), bf16[16,768,128]{2,1,0:T(8,128)(2,1)}, u32[]{:S(2)}, u32[]{:S(2)}) async-start(bf16[16,768,128]{2,1,0:T(8,128)(2,1)} %pack.1), calls=%async_computation | async-start | bytes 6291456 | tf_op jit(solution)/shard_map/all_to_all | solution.py:393
  29.1 3.0 %collective-permute-start.1 = (f32[8]{0:T(128)S(1)}, f32[8]{0:T(128)S(1)}, u32[]{:S(2)}, u32[]{:S(2)}) collective-permute-start(f32[8]{0:T(128)S(1)} %add.45), channel_id=1, source_target_pairs={{4,0},{5,1},{6,2},{7,3},{0,4},{1,5},{2,6},{3,7},{12,8},{13,9},{14,... | collective-permute-start | bytes 104 | tf_op jit(solution)/shard_map/ppermute | solution.py:54
  34.5 2.4 %collective-permute-done.3 = f32[8]{0:T(128)S(1)} collective-permute-done((f32[8]{0:T(128)S(1)}, f32[8]{0:T(128)S(1)}, u32[]{:S(2)}, u32[]{:S(2)}) %collective-permute-start.3) | collective-permute-done | bytes 64 | tf_op jit(solution)/shard_map/ppermute | solution.py:54
  36.9 2.8 %collective-permute-start.10 = (bf16[512,384]{1,0:T(8,128)(2,1)S(1)}, bf16[512,384]{1,0:T(8,128)(2,1)S(1)}, u32[]{:S(2)}, u32[]{:S(2)}) collective-permute-start(bf16[512,384]{1,0:T(8,128)(2,1)S(1)} %constant_dynamic-update-slice_fusion), channel_id=1, source_target_pairs={{64,0},{72,8},{80,16},{88,24},{96,32},{104,40},{112,48},{120,56},{... | collective-permute-start | bytes 1179656 | tf_op jit(solution)/shard_map/ppermute | solution.py:29
  40.0 2.4 %collective-permute-start.8 = (bf16[512,384]{1,0:T(8,128)(2,1)S(1)}, bf16[512,384]{1,0:T(8,128)(2,1)S(1)}, u32[]{:S(2)}, u32[]{:S(2)}) collective-permute-start(bf16[512,384]{1,0:T(8,128)(2,1)S(1)} %constant_dynamic-update-slice_fusion), channel_id=1, source_target_pairs={{32,0},{40,8},{48,16},{56,24},{64,32},{72,40},{80,48},{88,56},{96,... | collective-permute-start | bytes 1179656 | tf_op jit(solution)/shard_map/ppermute | solution.py:29
  42.4 11.2 %collective-permute-done.10 = bf16[512,384]{1,0:T(8,128)(2,1)S(1)} collective-permute-done((bf16[512,384]{1,0:T(8,128)(2,1)S(1)}, bf16[512,384]{1,0:T(8,128)(2,1)S(1)}, u32[]{:S(2)}, u32[]{:S(2)}) %collective-permute-start.10) | collective-permute-done | bytes 393248 | tf_op jit(solution)/shard_map/ppermute | solution.py:29
  53.7 13.6 %collective-permute-done.11 = bf16[512,384]{1,0:T(8,128)(2,1)S(1)} collective-permute-done((bf16[512,384]{1,0:T(8,128)(2,1)S(1)}, bf16[512,384]{1,0:T(8,128)(2,1)S(1)}, u32[]{:S(2)}, u32[]{:S(2)}) %collective-permute-start.11) | collective-permute-done | bytes 393248 | tf_op jit(solution)/shard_map/ppermute | solution.py:29
  68.8 1.5 collective-permute-start.9
  72.3 15.1 %collective-permute-done.12.rest_5_ = bf16[1024,384]{1,0:T(8,128)(2,1)S(1)} collective-permute-done((bf16[1024,384]{1,0:T(8,128)(2,1)S(1)}, bf16[1024,384]{1,0:T(8,128)(2,1)S(1)}, u32[]{:S(2)}, u32[]{:S(2)}) %collective-permute-start.12) | collective-permute-done | bytes 786464 | tf_op jit(solution)/shard_map/ppermute | solution.py:54
  90.3 11.5 %all-to-all-done.q_ref.kv_ref = bf16[16,768,128]{2,1,0:T(8,128)(2,1)} async-done(((bf16[16,768,128]{2,1,0:T(8,128)(2,1)}), bf16[16,768,128]{2,1,0:T(8,128)(2,1)}, u32[]{:S(2)}, u32[]{:S(2)}) %all-to-all-start) | async-done | bytes 3145760 | tf_op jit(solution)/shard_map/all_to_all | solution.py:393
  101.8 8.6 %all-to-all-start.1 = ((bf16[16,128,128]{2,1,0:T(8,128)(2,1)}), bf16[16,128,128]{2,1,0:T(8,128)(2,1)}, u32[]{:S(2)}, u32[]{:S(2)}) async-start(bf16[16,128,128]{2,1,0:T(8,128)(2,1)} %pack_queries.1), calls=%async_computation.1 | async-start | bytes 1048576 | tf_op jit(solution)/shard_map/all_to_all | solution.py:393
  110.4 11.3 %attention0.1.rest_0_ = bf16[16,256,128]{2,1,0:T(8,128)(2,1)} custom-call(bf16[16,768,128]{2,1,0:T(8,128)(2,1)} %all-to-all-done.q_ref.kv_ref, bf16[16,768,128]{2,1,0:T(8,128)(2,1)} %all-to-all-done.q_ref.kv_ref), custom_call_target="tpu_custom_call" | custom-call | flops 5368709120 | bytes 2359296 | tf_op jit(solution)/shard_map/attention0/pallas_call | solution.py:177
  121.7 5.5 %all-to-all-done.1.q_ref = bf16[16,128,128]{2,1,0:T(8,128)(2,1)} async-done(((bf16[16,128,128]{2,1,0:T(8,128)(2,1)}), bf16[16,128,128]{2,1,0:T(8,128)(2,1)}, u32[]{:S(2)}, u32[]{:S(2)}) %all-to-all-start.1) | async-done | bytes 524320 | tf_op jit(solution)/shard_map/all_to_all | solution.py:393
  127.2 11.3 %attention1.1 = bf16[16,256,128]{2,1,0:T(8,128)(2,1)} custom-call(bf16[16,128,128]{2,1,0:T(8,128)(2,1)} %all-to-all-done.1.q_ref, bf16[16,768,128]{2,1,0:T(8,128)(2,1)} %all-to-all-done.q_ref.kv_ref, bf16[16,256,128]{2,1,0:T(8,128)(2,1)} %attention0.1.rest_0_), custom_call_target="tpu_custom_call", output_to_operand_aliasing={{}: (2, {})} | custom-call | flops 5368709120 | bytes 2359296 | tf_op jit(solution)/shard_map/attention1/pallas_call | solution.py:177
  138.5 6.2 %all-to-all-start.2 = ((bf16[16,256,128]{2,1,0:T(8,128)(2,1)}), bf16[16,256,128]{2,1,0:T(8,128)(2,1)}, u32[]{:S(2)}, u32[]{:S(2)}) async-start(bf16[16,256,128]{2,1,0:T(8,128)(2,1)} %attention1.1), calls=%async_computation.2 | async-start | bytes 2097152 | tf_op jit(solution)/shard_map/all_to_all | solution.py:393
  144.8 2.7 %collective-permute-start.17 = (bf16[1024,384]{1,0:T(8,128)(2,1)S(1)}, bf16[1024,384]{1,0:T(8,128)(2,1)}, u32[]{:S(2)}, u32[]{:S(2)}) collective-permute-start(bf16[1024,384]{1,0:T(8,128)(2,1)S(1)} %collective-permute-done.9.rest_2_), channel_id=1, source_target_pairs={{2,0},{3,1},{4,2},{5,3},{6,4},{7,5},{0,6},{1,7},{10,8},{11,9},{12,... | collective-permute-start | bytes 2359304 | tf_op jit(solution)/shard_map/ppermute | solution.py:54
  147.5 3.3 %collective-permute-start.22 = (bf16[1024,384]{1,0:T(8,128)(2,1)}, bf16[1024,384]{1,0:T(8,128)(2,1)}, u32[]{:S(2)}, u32[]{:S(2)}) collective-permute-start(bf16[1024,384]{1,0:T(8,128)(2,1)} %copy-done.7), channel_id=1, source_target_pairs={{0,128},{128,0},{1,129},{129,1},{2,130},{130,2},{3,131},{131,3},{4... | collective-permute-start | bytes 2359304 | tf_op jit(solution)/shard_map/ppermute | solution.py:63
  151.4 11.2 %collective-permute-done.18.rest_7_ = bf16[1024,384]{1,0:T(8,128)(2,1)} collective-permute-done((bf16[1024,384]{1,0:T(8,128)(2,1)}, bf16[1024,384]{1,0:T(8,128)(2,1)}, u32[]{:S(2)}, u32[]{:S(2)}) %collective-permute-start.18) | collective-permute-done | bytes 786464 | tf_op jit(solution)/shard_map/ppermute | solution.py:54
  162.6 3.7 %collective-permute-start.21 = (bf16[1024,384]{1,0:T(8,128)(2,1)}, bf16[1024,384]{1,0:T(8,128)(2,1)}, u32[]{:S(2)}, u32[]{:S(2)}) collective-permute-start(bf16[1024,384]{1,0:T(8,128)(2,1)} %collective-permute-done.16.rest_4_), channel_id=1, source_target_pairs={{0,128},{128,0},{1,129},{129,1},{2,130},{130,2},{3,131},{131,3},{4... | collective-permute-start | bytes 2359304 | tf_op jit(solution)/shard_map/ppermute | solution.py:63
  170.8 10.8 %hidden.1 = (bf16[256,3072]{1,0:T(8,128)(2,1)}, f32[64,256]{1,0:T(8,128)S(1)}) custom-call(s32[4]{0:T(128)S(1)} %pad_add_fusion.place, bf16[16,256,128]{2,1,0:T(8,128)(2,1)} %all-to-all-done.2.heads_ref, bf16[1,2,128,3072]{3,2,1,0:T(8,128)(2,1)} %state_any.1, bf16[3,2,3072]{2,1,0:T(2,128)(2,1)S(1)} %bitcast.21, bf16[64,3072]{1,0:T(8,128)(2,1)S(1)} %bitcast.18, ...), custom_call_target="tpu_custom_call" | custom-call | flops 3221225472 | bytes 12582912 | tf_op jit(solution)/shard_map/hidden/pallas_call | solution.py:279
  187.5 15.5 %all_to_all.20.parts_ref = f32[8,32,384]{2,1,0:T(8,128)} all-to-all(f32[8,32,384]{2,1,0:T(8,128)S(1)} %add.49), channel_id=1, replica_groups=mesh['cfg'=2,'seq'=16,'dp'=8] {'dp'}, dimensions={0} | all-to-all | bytes 786432 | tf_op jit(solution)/shard_map/all_to_all | solution.py:484
  203.0 1.6 fold.1
  204.7 4.8 %collective-permute-start.27 = (f32[40,384]{1,0:T(8,128)}, f32[40,384]{1,0:T(8,128)S(1)}, u32[]{:S(2)}, u32[]{:S(2)}) collective-permute-start(f32[40,384]{1,0:T(8,128)} %fold.1), channel_id=1, source_target_pairs={{16,0},{24,8},{0,16},{8,24},{48,32},{56,40},{32,48},{40,56},{80,64... | collective-permute-start | bytes 184328 | tf_op jit(solution)/shard_map/ppermute | solution.py:49
  209.7 2.1 collective-permute-start.29
  211.9 4.2 %collective-permute-done.28 = f32[40,384]{1,0:T(8,128)S(1)} collective-permute-done((f32[40,384]{1,0:T(8,128)}, f32[40,384]{1,0:T(8,128)S(1)}, u32[]{:S(2)}, u32[]{:S(2)}) %collective-permute-start.28) | collective-permute-done | bytes 61472 | tf_op jit(solution)/shard_map/ppermute | solution.py:49
  217.0 3.0 %collective-permute-start.30 = (f32[40,384]{1,0:T(8,128)S(1)}, f32[40,384]{1,0:T(8,128)S(1)}, u32[]{:S(2)}, u32[]{:S(2)}) collective-permute-start(f32[40,384]{1,0:T(8,128)S(1)} %add_add_fusion.1), channel_id=1, source_target_pairs={{64,0},{72,8},{80,16},{88,24},{96,32},{104,40},{112,48},{120,56},{... | collective-permute-start | bytes 184328 | tf_op jit(solution)/shard_map/ppermute | solution.py:29
  223.0 2.4 %collective-permute-done.32 = f32[40,384]{1,0:T(8,128)S(1)} collective-permute-done((f32[40,384]{1,0:T(8,128)S(1)}, f32[40,384]{1,0:T(8,128)S(1)}, u32[]{:S(2)}, u32[]{:S(2)}) %collective-permute-start.32) | collective-permute-done | bytes 61472 | tf_op jit(solution)/shard_map/ppermute | solution.py:29
  225.4 4.3 %collective-permute-start.33 = (f32[40,384]{1,0:T(8,128)S(1)}, f32[40,384]{1,0:T(8,128)S(1)}, u32[]{:S(2)}, u32[]{:S(2)}) collective-permute-start(f32[40,384]{1,0:T(8,128)S(1)} %add_add_fusion), channel_id=1, source_target_pairs={{0,128},{128,0},{1,129},{129,1},{2,130},{130,2},{3,131},{131,3},{4... | collective-permute-start | bytes 184328 | tf_op jit(solution)/shard_map/ppermute | solution.py:63
  (98 shorter events, 31.1 us)
Async XLA Ops:
  0.6 18.3 %collective-permute-start.4 = (bf16[128,384]{1,0:T(8,128)(2,1)}, bf16[128,384]{1,0:T(8,128)(2,1)S(1)}, u32[]{:S(2)}, u32[]{:S(2)}) collective-permute-start(bf16[128,384]{1,0:T(8,128)(2,1)} %param.13), channel_id=1, source_target_pairs={{0,0},{128,1},{2,2},{130,3},{4,4},{132,5},{6,6},{134,7},{8,8},{136... | collective-permute-start | bytes 294920 | tf_op jit(solution)/shard_map/ppermute | solution.py:44
  5.6 13.4 %collective-permute-start.5 = (bf16[128,384]{1,0:T(8,128)(2,1)}, bf16[128,384]{1,0:T(8,128)(2,1)S(1)}, u32[]{:S(2)}, u32[]{:S(2)}) collective-permute-start(bf16[128,384]{1,0:T(8,128)(2,1)} %param.13), channel_id=1, source_target_pairs={{8,0},{136,1},{10,2},{138,3},{12,4},{140,5},{14,6},{142,7},{16,8},... | collective-permute-start | bytes 294920 | tf_op jit(solution)/shard_map/ppermute | solution.py:44
  10.0 10.1 %collective-permute-start.6 = (bf16[128,384]{1,0:T(8,128)(2,1)}, bf16[128,384]{1,0:T(8,128)(2,1)S(1)}, u32[]{:S(2)}, u32[]{:S(2)}) collective-permute-start(bf16[128,384]{1,0:T(8,128)(2,1)} %param.13), channel_id=1, source_target_pairs={{16,0},{144,1},{18,2},{146,3},{20,4},{148,5},{22,6},{150,7},{24,8}... | collective-permute-start | bytes 294920 | tf_op jit(solution)/shard_map/ppermute | solution.py:44
  12.2 9.4 %collective-permute-start.7 = (bf16[128,384]{1,0:T(8,128)(2,1)}, bf16[128,384]{1,0:T(8,128)(2,1)S(1)}, u32[]{:S(2)}, u32[]{:S(2)}) collective-permute-start(bf16[128,384]{1,0:T(8,128)(2,1)} %param.13), channel_id=1, source_target_pairs={{24,0},{152,1},{26,2},{154,3},{28,4},{156,5},{30,6},{158,7},{0,8},... | collective-permute-start | bytes 294920 | tf_op jit(solution)/shard_map/ppermute | solution.py:44
  14.3 4.6 %collective-permute-start = (f32[8]{0:T(128)S(1)}, f32[8]{0:T(128)S(1)}, u32[]{:S(2)}, u32[]{:S(2)}) collective-permute-start(f32[8]{0:T(128)S(1)} %select_reduce_fusion.1), channel_id=1, source_target_pairs={{1,0},{0,1},{3,2},{2,3},{5,4},{4,5},{7,6},{6,7},{9,8},{8,9},{11,10... | collective-permute-start | bytes 104 | tf_op jit(solution)/shard_map/ppermute | solution.py:59
  21.6 80.1 %all-to-all-start = ((bf16[16,768,128]{2,1,0:T(8,128)(2,1)}), bf16[16,768,128]{2,1,0:T(8,128)(2,1)}, u32[]{:S(2)}, u32[]{:S(2)}) async-start(bf16[16,768,128]{2,1,0:T(8,128)(2,1)} %pack.1), calls=%async_computation | async-start | bytes 6291456 | tf_op jit(solution)/shard_map/all_to_all | solution.py:393
  29.1 4.4 %collective-permute-start.1 = (f32[8]{0:T(128)S(1)}, f32[8]{0:T(128)S(1)}, u32[]{:S(2)}, u32[]{:S(2)}) collective-permute-start(f32[8]{0:T(128)S(1)} %add.45), channel_id=1, source_target_pairs={{4,0},{5,1},{6,2},{7,3},{0,4},{1,5},{2,6},{3,7},{12,8},{13,9},{14,... | collective-permute-start | bytes 104 | tf_op jit(solution)/shard_map/ppermute | solution.py:54
  32.9 4.0 %collective-permute-start.3 = (f32[8]{0:T(128)S(1)}, f32[8]{0:T(128)S(1)}, u32[]{:S(2)}, u32[]{:S(2)}) collective-permute-start(f32[8]{0:T(128)S(1)} %add.45), channel_id=1, source_target_pairs={{6,0},{7,1},{0,2},{1,3},{2,4},{3,5},{4,6},{5,7},{14,8},{15,9},{8,1... | collective-permute-start | bytes 104 | tf_op jit(solution)/shard_map/ppermute | solution.py:54
  36.9 16.7 %collective-permute-start.10 = (bf16[512,384]{1,0:T(8,128)(2,1)S(1)}, bf16[512,384]{1,0:T(8,128)(2,1)S(1)}, u32[]{:S(2)}, u32[]{:S(2)}) collective-permute-start(bf16[512,384]{1,0:T(8,128)(2,1)S(1)} %constant_dynamic-update-slice_fusion), channel_id=1, source_target_pairs={{64,0},{72,8},{80,16},{88,24},{96,32},{104,40},{112,48},{120,56},{... | collective-permute-start | bytes 1179656 | tf_op jit(solution)/shard_map/ppermute | solution.py:29
  39.7 27.5 %collective-permute-start.11 = (bf16[512,384]{1,0:T(8,128)(2,1)S(1)}, bf16[512,384]{1,0:T(8,128)(2,1)S(1)}, u32[]{:S(2)}, u32[]{:S(2)}) collective-permute-start(bf16[512,384]{1,0:T(8,128)(2,1)S(1)} %constant_dynamic-update-slice_fusion), channel_id=1, source_target_pairs={{96,0},{104,8},{112,16},{120,24},{0,32},{8,40},{16,48},{24,56},{32... | collective-permute-start | bytes 1179656 | tf_op jit(solution)/shard_map/ppermute | solution.py:29
  40.0 28.7 %collective-permute-start.8 = (bf16[512,384]{1,0:T(8,128)(2,1)S(1)}, bf16[512,384]{1,0:T(8,128)(2,1)S(1)}, u32[]{:S(2)}, u32[]{:S(2)}) collective-permute-start(bf16[512,384]{1,0:T(8,128)(2,1)S(1)} %constant_dynamic-update-slice_fusion), channel_id=1, source_target_pairs={{32,0},{40,8},{48,16},{56,24},{64,32},{72,40},{80,48},{88,56},{96,... | collective-permute-start | bytes 1179656 | tf_op jit(solution)/shard_map/ppermute | solution.py:29
  67.3 20.1 %collective-permute-start.12 = (bf16[1024,384]{1,0:T(8,128)(2,1)S(1)}, bf16[1024,384]{1,0:T(8,128)(2,1)S(1)}, u32[]{:S(2)}, u32[]{:S(2)}) collective-permute-start(bf16[1024,384]{1,0:T(8,128)(2,1)S(1)} %constant_dynamic-update-slice_fusion.6.rest_1_), channel_id=1, source_target_pairs={{6,0},{7,1},{0,2},{1,3},{2,4},{3,5},{4,6},{5,7},{14,8},{15,9},{8,1... | collective-permute-start | bytes 2359304 | tf_op jit(solution)/shard_map/ppermute | solution.py:54
  68.8 20.6 %collective-permute-start.9 = (bf16[1024,384]{1,0:T(8,128)(2,1)S(1)}, bf16[1024,384]{1,0:T(8,128)(2,1)S(1)}, u32[]{:S(2)}, u32[]{:S(2)}) collective-permute-start(bf16[1024,384]{1,0:T(8,128)(2,1)S(1)} %constant_dynamic-update-slice_fusion.4.rest_0_), channel_id=1, source_target_pairs={{2,0},{3,1},{4,2},{5,3},{6,4},{7,5},{0,6},{1,7},{10,8},{11,9},{12,... | collective-permute-start | bytes 2359304 | tf_op jit(solution)/shard_map/ppermute | solution.py:54
  70.3 19.1 %collective-permute-start.14 = (bf16[1024,384]{1,0:T(8,128)(2,1)S(1)}, bf16[1024,384]{1,0:T(8,128)(2,1)S(1)}, u32[]{:S(2)}, u32[]{:S(2)}) collective-permute-start(bf16[1024,384]{1,0:T(8,128)(2,1)S(1)} %constant_dynamic-update-slice_fusion.6.rest_1_), channel_id=1, source_target_pairs={{0,128},{128,0},{1,129},{129,1},{2,130},{130,2},{3,131},{131,3},{4... | collective-permute-start | bytes 2359304 | tf_op jit(solution)/shard_map/ppermute | solution.py:63
  71.3 19.0 %collective-permute-start.13 = (bf16[1024,384]{1,0:T(8,128)(2,1)S(1)}, bf16[1024,384]{1,0:T(8,128)(2,1)}, u32[]{:S(2)}, u32[]{:S(2)}) collective-permute-start(bf16[1024,384]{1,0:T(8,128)(2,1)S(1)} %constant_dynamic-update-slice_fusion.4.rest_0_), channel_id=1, source_target_pairs={{0,128},{128,0},{1,129},{129,1},{2,130},{130,2},{3,131},{131,3},{4... | collective-permute-start | bytes 2359304 | tf_op jit(solution)/shard_map/ppermute | solution.py:63
  71.3 39.1 %collective-permute-start.15 = (bf16[1024,384]{1,0:T(8,128)(2,1)S(1)}, bf16[1024,384]{1,0:T(8,128)(2,1)}, u32[]{:S(2)}, u32[]{:S(2)}) collective-permute-start(bf16[1024,384]{1,0:T(8,128)(2,1)S(1)} %constant_dynamic-update-slice_fusion.6.rest_1_), channel_id=1, source_target_pairs={{2,0},{3,1},{4,2},{5,3},{6,4},{7,5},{0,6},{1,7},{10,8},{11,9},{12,... | collective-permute-start | bytes 2359304 | tf_op jit(solution)/shard_map/ppermute | solution.py:54
  88.3 22.1 %collective-permute-start.16 = (bf16[1024,384]{1,0:T(8,128)(2,1)S(1)}, bf16[1024,384]{1,0:T(8,128)(2,1)}, u32[]{:S(2)}, u32[]{:S(2)}) collective-permute-start(bf16[1024,384]{1,0:T(8,128)(2,1)S(1)} %constant_dynamic-update-slice_fusion.4.rest_0_), channel_id=1, source_target_pairs={{6,0},{7,1},{0,2},{1,3},{2,4},{3,5},{4,6},{5,7},{14,8},{15,9},{8,1... | collective-permute-start | bytes 2359304 | tf_op jit(solution)/shard_map/ppermute | solution.py:54
  101.8 25.4 %all-to-all-start.1 = ((bf16[16,128,128]{2,1,0:T(8,128)(2,1)}), bf16[16,128,128]{2,1,0:T(8,128)(2,1)}, u32[]{:S(2)}, u32[]{:S(2)}) async-start(bf16[16,128,128]{2,1,0:T(8,128)(2,1)} %pack_queries.1), calls=%async_computation.1 | async-start | bytes 1048576 | tf_op jit(solution)/shard_map/all_to_all | solution.py:393
  138.5 28.7 %all-to-all-start.2 = ((bf16[16,256,128]{2,1,0:T(8,128)(2,1)}), bf16[16,256,128]{2,1,0:T(8,128)(2,1)}, u32[]{:S(2)}, u32[]{:S(2)}) async-start(bf16[16,256,128]{2,1,0:T(8,128)(2,1)} %attention1.1), calls=%async_computation.2 | async-start | bytes 2097152 | tf_op jit(solution)/shard_map/all_to_all | solution.py:393
  144.7 17.9 %collective-permute-start.18 = (bf16[1024,384]{1,0:T(8,128)(2,1)}, bf16[1024,384]{1,0:T(8,128)(2,1)}, u32[]{:S(2)}, u32[]{:S(2)}) collective-permute-start(bf16[1024,384]{1,0:T(8,128)(2,1)} %copy-done.7), channel_id=1, source_target_pairs={{6,0},{7,1},{0,2},{1,3},{2,4},{3,5},{4,6},{5,7},{14,8},{15,9},{8,1... | collective-permute-start | bytes 2359304 | tf_op jit(solution)/shard_map/ppermute | solution.py:54
  144.8 21.5 %collective-permute-start.17 = (bf16[1024,384]{1,0:T(8,128)(2,1)S(1)}, bf16[1024,384]{1,0:T(8,128)(2,1)}, u32[]{:S(2)}, u32[]{:S(2)}) collective-permute-start(bf16[1024,384]{1,0:T(8,128)(2,1)S(1)} %collective-permute-done.9.rest_2_), channel_id=1, source_target_pairs={{2,0},{3,1},{4,2},{5,3},{6,4},{7,5},{0,6},{1,7},{10,8},{11,9},{12,... | collective-permute-start | bytes 2359304 | tf_op jit(solution)/shard_map/ppermute | solution.py:54
  147.5 18.8 %collective-permute-start.22 = (bf16[1024,384]{1,0:T(8,128)(2,1)}, bf16[1024,384]{1,0:T(8,128)(2,1)}, u32[]{:S(2)}, u32[]{:S(2)}) collective-permute-start(bf16[1024,384]{1,0:T(8,128)(2,1)} %copy-done.7), channel_id=1, source_target_pairs={{0,128},{128,0},{1,129},{129,1},{2,130},{130,2},{3,131},{131,3},{4... | collective-permute-start | bytes 2359304 | tf_op jit(solution)/shard_map/ppermute | solution.py:63
  150.8 16.4 %collective-permute-start.19 = (bf16[1024,384]{1,0:T(8,128)(2,1)S(1)}, bf16[1024,384]{1,0:T(8,128)(2,1)}, u32[]{:S(2)}, u32[]{:S(2)}) collective-permute-start(bf16[1024,384]{1,0:T(8,128)(2,1)S(1)} %collective-permute-done.9.rest_2_), channel_id=1, source_target_pairs={{0,128},{128,0},{1,129},{129,1},{2,130},{130,2},{3,131},{131,3},{4... | collective-permute-start | bytes 2359304 | tf_op jit(solution)/shard_map/ppermute | solution.py:63
  150.9 16.3 %collective-permute-start.20 = (bf16[1024,384]{1,0:T(8,128)(2,1)}, bf16[1024,384]{1,0:T(8,128)(2,1)}, u32[]{:S(2)}, u32[]{:S(2)}) collective-permute-start(bf16[1024,384]{1,0:T(8,128)(2,1)} %collective-permute-done.15.rest_3_), channel_id=1, source_target_pairs={{0,128},{128,0},{1,129},{129,1},{2,130},{130,2},{3,131},{131,3},{4... | collective-permute-start | bytes 2359304 | tf_op jit(solution)/shard_map/ppermute | solution.py:63
  162.6 5.9 %collective-permute-start.21 = (bf16[1024,384]{1,0:T(8,128)(2,1)}, bf16[1024,384]{1,0:T(8,128)(2,1)}, u32[]{:S(2)}, u32[]{:S(2)}) collective-permute-start(bf16[1024,384]{1,0:T(8,128)(2,1)} %collective-permute-done.16.rest_4_), channel_id=1, source_target_pairs={{0,128},{128,0},{1,129},{129,1},{2,130},{130,2},{3,131},{131,3},{4... | collective-permute-start | bytes 2359304 | tf_op jit(solution)/shard_map/ppermute | solution.py:63
  166.3 4.5 %collective-permute-start.23 = (bf16[1024,384]{1,0:T(8,128)(2,1)}, bf16[1024,384]{1,0:T(8,128)(2,1)}, u32[]{:S(2)}, u32[]{:S(2)}) collective-permute-start(bf16[1024,384]{1,0:T(8,128)(2,1)} %collective-permute-done.17.rest_6_), channel_id=1, source_target_pairs={{0,128},{128,0},{1,129},{129,1},{2,130},{130,2},{3,131},{131,3},{4... | collective-permute-start | bytes 2359304 | tf_op jit(solution)/shard_map/ppermute | solution.py:63
  204.7 7.3 %collective-permute-start.27 = (f32[40,384]{1,0:T(8,128)}, f32[40,384]{1,0:T(8,128)S(1)}, u32[]{:S(2)}, u32[]{:S(2)}) collective-permute-start(f32[40,384]{1,0:T(8,128)} %fold.1), channel_id=1, source_target_pairs={{16,0},{24,8},{0,16},{8,24},{48,32},{56,40},{32,48},{40,56},{80,64... | collective-permute-start | bytes 184328 | tf_op jit(solution)/shard_map/ppermute | solution.py:49
  209.5 6.6 %collective-permute-start.28 = (f32[40,384]{1,0:T(8,128)}, f32[40,384]{1,0:T(8,128)S(1)}, u32[]{:S(2)}, u32[]{:S(2)}) collective-permute-start(f32[40,384]{1,0:T(8,128)} %fold.1), channel_id=1, source_target_pairs={{8,0},{16,8},{24,16},{0,24},{40,32},{48,40},{56,48},{32,56},{72,64... | collective-permute-start | bytes 184328 | tf_op jit(solution)/shard_map/ppermute | solution.py:49
  209.7 6.4 %collective-permute-start.29 = (f32[40,384]{1,0:T(8,128)}, f32[40,384]{1,0:T(8,128)S(1)}, u32[]{:S(2)}, u32[]{:S(2)}) collective-permute-start(f32[40,384]{1,0:T(8,128)} %fold.1), channel_id=1, source_target_pairs={{24,0},{0,8},{8,16},{16,24},{56,32},{32,40},{40,48},{48,56},{88,64... | collective-permute-start | bytes 184328 | tf_op jit(solution)/shard_map/ppermute | solution.py:49
  217.0 4.7 %collective-permute-start.30 = (f32[40,384]{1,0:T(8,128)S(1)}, f32[40,384]{1,0:T(8,128)S(1)}, u32[]{:S(2)}, u32[]{:S(2)}) collective-permute-start(f32[40,384]{1,0:T(8,128)S(1)} %add_add_fusion.1), channel_id=1, source_target_pairs={{64,0},{72,8},{80,16},{88,24},{96,32},{104,40},{112,48},{120,56},{... | collective-permute-start | bytes 184328 | tf_op jit(solution)/shard_map/ppermute | solution.py:29
  220.8 4.6 %collective-permute-start.32 = (f32[40,384]{1,0:T(8,128)S(1)}, f32[40,384]{1,0:T(8,128)S(1)}, u32[]{:S(2)}, u32[]{:S(2)}) collective-permute-start(f32[40,384]{1,0:T(8,128)S(1)} %add_add_fusion.1), channel_id=1, source_target_pairs={{96,0},{104,8},{112,16},{120,24},{0,32},{8,40},{16,48},{24,56},{32... | collective-permute-start | bytes 184328 | tf_op jit(solution)/shard_map/ppermute | solution.py:29
  225.4 5.2 %collective-permute-start.33 = (f32[40,384]{1,0:T(8,128)S(1)}, f32[40,384]{1,0:T(8,128)S(1)}, u32[]{:S(2)}, u32[]{:S(2)}) collective-permute-start(f32[40,384]{1,0:T(8,128)S(1)} %add_add_fusion), channel_id=1, source_target_pairs={{0,128},{128,0},{1,129},{129,1},{2,130},{130,2},{3,131},{131,3},{4... | collective-permute-start | bytes 184328 | tf_op jit(solution)/shard_map/ppermute | solution.py:63
  (17 other events, 319.5 us)

commit v2 on v1

--- a/solution.py
+++ b/solution.py
@@ -465,7 +465,7 @@
         ]
     )
 
-    returned = after(exchange(attended), terms)
+    returned = after(exchange(after(attended, far_first, far_second)), terms)
     hidden, velocity = hidden_rows(
         place, returned, image_state, modulation[0].transpose(1, 0, 2), final_weight.T, pieces
     )

time: 232 us -> 229 us (0.987)
  starting transfers between devices: 78.2 us -> 73.6 us
    all_to_all x3, waiting for transfers between devices: 17 us -> 31.1 us  [exchange(): return lax.all_to_all(send, 'seq', split_axis=0, concat_axis=0, tiled=True)]
    ppermute x9, waiting for transfers between devices: 29.6 us -> 18.4 us  [from_y(): return lax.ppermute(value, 'dp', pairs)]
    ppermute x3, starting transfers between devices: 7.18 us -> 2.65 us  [from_zh(): return lax.ppermute(value, 'seq', pairs)]
    ppermute x11, waiting for transfers between devices: 6.14 us -> 3.67 us  [from_cfg(): return lax.ppermute(value, 'cfg', [(0, 1), (1, 0)])]
  transfers between devices with their start and end apart: 37 -> 37, of which waited for: 22 -> 19; matrix products, arithmetic and copies ran while one was open for 1% -> 1% of each run, Pallas kernels for 7% -> 12%
where the time goes in v2:
time: 229 us
  waiting for transfers between devices  90.6 us (40%)
  starting transfers between devices  73.6 us (32%)
  Pallas kernels  41.5 us (18%)
  blocking collectives  16.2 us (7%)
  other arithmetic  3.28 us (1%)
  local copies, waits for them, and re-layouts  2.61 us (1%)
    all_to_all x3, waiting for transfers between devices, exchange(): return lax.all_to_all(send, 'seq', split_axis=0, concat_axis=0, tiled=True)  31.1 us
    ppermute x6, waiting for transfers between devices, from_x(): return lax.ppermute(value, 'seq', pairs)  29.1 us
    all_to_all x3, starting transfers between devices, exchange(): return lax.all_to_all(send, 'seq', split_axis=0, concat_axis=0, tiled=True)  23.6 us
    pallas_call x2, Pallas kernels, attention(): pl.pallas_call(attention_kernel, grid=(ATTENTION_STEPS,), in_specs=[pl.Bl...  22.5 us
    ppermute x9, waiting for transfers between devices, from_y(): return lax.ppermute(value, 'dp', pairs)  18.4 us
    all_to_all x1, blocking collectives, per_device(): lax.all_to_all(kept, 'dp', split_axis=0, concat_axis=0, tiled=True)  16.2 us
    ppermute x11, starting transfers between devices, from_cfg(): return lax.ppermute(value, 'cfg', [(0, 1), (1, 0)])  14.2 us
    ppermute x4, starting transfers between devices, from_column(): return lax.ppermute(value, ('cfg', 'seq', 'dp'), pairs)  12.9 us
  transfers between devices with their start and end apart: 37, of which 19 were waited for; matrix products, arithmetic and copies ran while one was open for 1% of the time, Pallas kernels for 12%

profile of v2, /device:TPU:1, one launch (start us, length us, event | category | flops | bytes accessed | tf_op | source)
XLA Modules:
  0.0 228.7 jit_solution(12021727441198485232)
XLA Ops:
  0.6 4.9 %collective-permute-start.4 = (bf16[128,384]{1,0:T(8,128)(2,1)}, bf16[128,384]{1,0:T(8,128)(2,1)S(1)}, u32[]{:S(2)}, u32[]{:S(2)}) collective-permute-start(bf16[128,384]{1,0:T(8,128)(2,1)} %param.13), channel_id=1, source_target_pairs={{0,0},{128,1},{2,2},{130,3},{4,4},{132,5},{6,6},{134,7},{8,8},{136... | collective-permute-start | bytes 294920 | tf_op jit(solution)/shard_map/ppermute | solution.py:44
  5.6 4.5 %collective-permute-start.5 = (bf16[128,384]{1,0:T(8,128)(2,1)}, bf16[128,384]{1,0:T(8,128)(2,1)S(1)}, u32[]{:S(2)}, u32[]{:S(2)}) collective-permute-start(bf16[128,384]{1,0:T(8,128)(2,1)} %param.13), channel_id=1, source_target_pairs={{8,0},{136,1},{10,2},{138,3},{12,4},{140,5},{14,6},{142,7},{16,8},... | collective-permute-start | bytes 294920 | tf_op jit(solution)/shard_map/ppermute | solution.py:44
  10.0 2.2 collective-permute-start.6
  14.4 4.4 %pack.1 = bf16[16,768,128]{2,1,0:T(8,128)(2,1)} custom-call(bf16[1,2,128,6144]{3,2,1,0:T(8,128)(2,1)} %q_ref.3, bf16[1,2,128,6144]{3,2,1,0:T(8,128)(2,1)} %q_ref.3, bf16[1,2,32,4096]{3,2,1,0:T(8,128)(2,1)} %vt_ref.1, bf16[1,2,32,4096]{3,2,1,0:T(8,128)(2,1)} %vt_ref.1, bf16[1,2,128,6144]{3,2,1,0:T(8,128)(2,1)} %q_ref.3), custom_call_target="tpu_custom_call" | custom-call | bytes 6291456 | tf_op jit(solution)/shard_map/pack/pallas_call | solution.py:110
  20.1 1.5 collective-permute-done.7
  21.6 7.5 %all-to-all-start = ((bf16[16,768,128]{2,1,0:T(8,128)(2,1)}), bf16[16,768,128]{2,1,0:T(8,128)(2,1)}, u32[]{:S(2)}, u32[]{:S(2)}) async-start(bf16[16,768,128]{2,1,0:T(8,128)(2,1)} %pack.1), calls=%async_computation | async-start | bytes 6291456 | tf_op jit(solution)/shard_map/all_to_all | solution.py:393
  29.1 3.0 %collective-permute-start.1 = (f32[8]{0:T(128)S(1)}, f32[8]{0:T(128)S(1)}, u32[]{:S(2)}, u32[]{:S(2)}) collective-permute-start(f32[8]{0:T(128)S(1)} %add.45), channel_id=1, source_target_pairs={{4,0},{5,1},{6,2},{7,3},{0,4},{1,5},{2,6},{3,7},{12,8},{13,9},{14,... | collective-permute-start | bytes 104 | tf_op jit(solution)/shard_map/ppermute | solution.py:54
  34.5 2.4 %collective-permute-done.3 = f32[8]{0:T(128)S(1)} collective-permute-done((f32[8]{0:T(128)S(1)}, f32[8]{0:T(128)S(1)}, u32[]{:S(2)}, u32[]{:S(2)}) %collective-permute-start.3) | collective-permute-done | bytes 64 | tf_op jit(solution)/shard_map/ppermute | solution.py:54
  36.9 2.8 %collective-permute-start.10 = (bf16[512,384]{1,0:T(8,128)(2,1)S(1)}, bf16[512,384]{1,0:T(8,128)(2,1)S(1)}, u32[]{:S(2)}, u32[]{:S(2)}) collective-permute-start(bf16[512,384]{1,0:T(8,128)(2,1)S(1)} %constant_dynamic-update-slice_fusion), channel_id=1, source_target_pairs={{64,0},{72,8},{80,16},{88,24},{96,32},{104,40},{112,48},{120,56},{... | collective-permute-start | bytes 1179656 | tf_op jit(solution)/shard_map/ppermute | solution.py:29
  40.0 2.4 %collective-permute-start.8 = (bf16[512,384]{1,0:T(8,128)(2,1)S(1)}, bf16[512,384]{1,0:T(8,128)(2,1)S(1)}, u32[]{:S(2)}, u32[]{:S(2)}) collective-permute-start(bf16[512,384]{1,0:T(8,128)(2,1)S(1)} %constant_dynamic-update-slice_fusion), channel_id=1, source_target_pairs={{32,0},{40,8},{48,16},{56,24},{64,32},{72,40},{80,48},{88,56},{96,... | collective-permute-start | bytes 1179656 | tf_op jit(solution)/shard_map/ppermute | solution.py:29
  42.4 11.2 %collective-permute-done.10 = bf16[512,384]{1,0:T(8,128)(2,1)S(1)} collective-permute-done((bf16[512,384]{1,0:T(8,128)(2,1)S(1)}, bf16[512,384]{1,0:T(8,128)(2,1)S(1)}, u32[]{:S(2)}, u32[]{:S(2)}) %collective-permute-start.10) | collective-permute-done | bytes 393248 | tf_op jit(solution)/shard_map/ppermute | solution.py:29
  53.7 13.6 %collective-permute-done.11 = bf16[512,384]{1,0:T(8,128)(2,1)S(1)} collective-permute-done((bf16[512,384]{1,0:T(8,128)(2,1)S(1)}, bf16[512,384]{1,0:T(8,128)(2,1)S(1)}, u32[]{:S(2)}, u32[]{:S(2)}) %collective-permute-start.11) | collective-permute-done | bytes 393248 | tf_op jit(solution)/shard_map/ppermute | solution.py:29
  68.8 1.5 collective-permute-start.9
  72.3 15.1 %collective-permute-done.12.rest_5_ = bf16[1024,384]{1,0:T(8,128)(2,1)} collective-permute-done((bf16[1024,384]{1,0:T(8,128)(2,1)S(1)}, bf16[1024,384]{1,0:T(8,128)(2,1)}, u32[]{:S(2)}, u32[]{:S(2)}) %collective-permute-start.12) | collective-permute-done | bytes 786464 | tf_op jit(solution)/shard_map/ppermute | solution.py:54
  89.4 12.3 %all-to-all-done.q_ref.kv_ref = bf16[16,768,128]{2,1,0:T(8,128)(2,1)} async-done(((bf16[16,768,128]{2,1,0:T(8,128)(2,1)}), bf16[16,768,128]{2,1,0:T(8,128)(2,1)}, u32[]{:S(2)}, u32[]{:S(2)}) %all-to-all-start) | async-done | bytes 3145760 | tf_op jit(solution)/shard_map/all_to_all | solution.py:393
  101.8 8.6 %all-to-all-start.1 = ((bf16[16,128,128]{2,1,0:T(8,128)(2,1)}), bf16[16,128,128]{2,1,0:T(8,128)(2,1)}, u32[]{:S(2)}, u32[]{:S(2)}) async-start(bf16[16,128,128]{2,1,0:T(8,128)(2,1)} %pack_queries.1), calls=%async_computation.1 | async-start | bytes 1048576 | tf_op jit(solution)/shard_map/all_to_all | solution.py:393
  110.4 1.7 collective-permute-start.18
  113.3 11.3 %attention0.1.rest_0_ = bf16[16,256,128]{2,1,0:T(8,128)(2,1)} custom-call(bf16[16,768,128]{2,1,0:T(8,128)(2,1)} %all-to-all-done.q_ref.kv_ref, bf16[16,768,128]{2,1,0:T(8,128)(2,1)} %all-to-all-done.q_ref.kv_ref), custom_call_target="tpu_custom_call" | custom-call | flops 5368709120 | bytes 2359296 | tf_op jit(solution)/shard_map/attention0/pallas_call | solution.py:177
  126.1 11.3 %attention1.1 = bf16[16,256,128]{2,1,0:T(8,128)(2,1)} custom-call(bf16[16,128,128]{2,1,0:T(8,128)(2,1)} %all-to-all-done.1.q_ref, bf16[16,768,128]{2,1,0:T(8,128)(2,1)} %all-to-all-done.q_ref.kv_ref, bf16[16,256,128]{2,1,0:T(8,128)(2,1)} %attention0.1.rest_0_), custom_call_target="tpu_custom_call", output_to_operand_aliasing={{}: (2, {})} | custom-call | flops 5368709120 | bytes 2359296 | tf_op jit(solution)/shard_map/attention1/pallas_call | solution.py:177
  137.4 7.5 %all-to-all-start.2 = ((bf16[16,256,128]{2,1,0:T(8,128)(2,1)}), bf16[16,256,128]{2,1,0:T(8,128)(2,1)}, u32[]{:S(2)}, u32[]{:S(2)}) async-start(bf16[16,256,128]{2,1,0:T(8,128)(2,1)} %attention1.1), calls=%async_computation.2 | async-start | bytes 2097152 | tf_op jit(solution)/shard_map/all_to_all | solution.py:393
  144.9 2.1 collective-permute-start.22
  150.0 17.4 %all-to-all-done.2.heads_ref = bf16[16,256,128]{2,1,0:T(8,128)(2,1)} async-done(((bf16[16,256,128]{2,1,0:T(8,128)(2,1)}), bf16[16,256,128]{2,1,0:T(8,128)(2,1)}, u32[]{:S(2)}, u32[]{:S(2)}) %all-to-all-start.2) | async-done | bytes 1048608 | tf_op jit(solution)/shard_map/all_to_all | solution.py:393
  167.4 10.8 %hidden.1 = (bf16[256,3072]{1,0:T(8,128)(2,1)}, f32[64,256]{1,0:T(8,128)S(1)}) custom-call(s32[4]{0:T(128)S(1)} %pad_add_fusion.place, bf16[16,256,128]{2,1,0:T(8,128)(2,1)} %all-to-all-done.2.heads_ref, bf16[1,2,128,3072]{3,2,1,0:T(8,128)(2,1)} %state_any.1, bf16[3,2,3072]{2,1,0:T(2,128)(2,1)S(1)} %bitcast.21, bf16[64,3072]{1,0:T(8,128)(2,1)S(1)} %bitcast.18, ...), custom_call_target="tpu_custom_call" | custom-call | flops 3221225472 | bytes 12582912 | tf_op jit(solution)/shard_map/hidden/pallas_call | solution.py:279
  178.2 4.2 %collective-permute-start.25 = (f32[64,256]{1,0:T(8,128)S(1)}, f32[64,256]{1,0:T(8,128)S(1)}, u32[]{:S(2)}, u32[]{:S(2)}) collective-permute-start(f32[64,256]{1,0:T(8,128)S(1)} %get-tuple-element.19.own_ref), channel_id=1, source_target_pairs={{0,128},{128,0},{1,129},{129,1},{2,130},{130,2},{3,131},{131,3},{4... | collective-permute-start | bytes 196616 | tf_op jit(solution)/shard_map/ppermute | solution.py:63
  187.6 16.2 %all_to_all.20.parts_ref = f32[8,32,384]{2,1,0:T(8,128)} all-to-all(f32[8,32,384]{2,1,0:T(8,128)S(1)} %add.49), channel_id=1, replica_groups=mesh['cfg'=2,'seq'=16,'dp'=8] {'dp'}, dimensions={0} | all-to-all | bytes 786432 | tf_op jit(solution)/shard_map/all_to_all | solution.py:484
  203.9 1.6 fold.1
  205.7 2.4 %collective-permute-start.28 = (f32[40,384]{1,0:T(8,128)}, f32[40,384]{1,0:T(8,128)S(1)}, u32[]{:S(2)}, u32[]{:S(2)}) collective-permute-start(f32[40,384]{1,0:T(8,128)} %fold.1), channel_id=1, source_target_pairs={{8,0},{16,8},{24,16},{0,24},{40,32},{48,40},{56,48},{32,56},{72,64... | collective-permute-start | bytes 184328 | tf_op jit(solution)/shard_map/ppermute | solution.py:49
  208.1 4.6 %collective-permute-done.27 = f32[40,384]{1,0:T(8,128)S(1)} collective-permute-done((f32[40,384]{1,0:T(8,128)}, f32[40,384]{1,0:T(8,128)S(1)}, u32[]{:S(2)}, u32[]{:S(2)}) %collective-permute-start.27) | collective-permute-done | bytes 61472 | tf_op jit(solution)/shard_map/ppermute | solution.py:49
  214.6 1.8 collective-permute-start.30
  216.4 1.5 collective-permute-start.31
  219.4 2.7 %collective-permute-done.32 = f32[40,384]{1,0:T(8,128)S(1)} collective-permute-done((f32[40,384]{1,0:T(8,128)S(1)}, f32[40,384]{1,0:T(8,128)S(1)}, u32[]{:S(2)}, u32[]{:S(2)}) %collective-permute-start.32) | collective-permute-done | bytes 61472 | tf_op jit(solution)/shard_map/ppermute | solution.py:29
  222.2 5.0 %collective-permute-start.33 = (f32[40,384]{1,0:T(8,128)S(1)}, f32[40,384]{1,0:T(8,128)S(1)}, u32[]{:S(2)}, u32[]{:S(2)}) collective-permute-start(f32[40,384]{1,0:T(8,128)S(1)} %add_add_fusion), channel_id=1, source_target_pairs={{0,128},{128,0},{1,129},{129,1},{2,130},{130,2},{3,131},{131,3},{4... | collective-permute-start | bytes 184328 | tf_op jit(solution)/shard_map/ppermute | solution.py:63
  (96 shorter events, 27.9 us)
Async XLA Ops:
  0.6 18.2 %collective-permute-start.4 = (bf16[128,384]{1,0:T(8,128)(2,1)}, bf16[128,384]{1,0:T(8,128)(2,1)S(1)}, u32[]{:S(2)}, u32[]{:S(2)}) collective-permute-start(bf16[128,384]{1,0:T(8,128)(2,1)} %param.13), channel_id=1, source_target_pairs={{0,0},{128,1},{2,2},{130,3},{4,4},{132,5},{6,6},{134,7},{8,8},{136... | collective-permute-start | bytes 294920 | tf_op jit(solution)/shard_map/ppermute | solution.py:44
  5.6 13.3 %collective-permute-start.5 = (bf16[128,384]{1,0:T(8,128)(2,1)}, bf16[128,384]{1,0:T(8,128)(2,1)S(1)}, u32[]{:S(2)}, u32[]{:S(2)}) collective-permute-start(bf16[128,384]{1,0:T(8,128)(2,1)} %param.13), channel_id=1, source_target_pairs={{8,0},{136,1},{10,2},{138,3},{12,4},{140,5},{14,6},{142,7},{16,8},... | collective-permute-start | bytes 294920 | tf_op jit(solution)/shard_map/ppermute | solution.py:44
  10.0 10.1 %collective-permute-start.6 = (bf16[128,384]{1,0:T(8,128)(2,1)}, bf16[128,384]{1,0:T(8,128)(2,1)S(1)}, u32[]{:S(2)}, u32[]{:S(2)}) collective-permute-start(bf16[128,384]{1,0:T(8,128)(2,1)} %param.13), channel_id=1, source_target_pairs={{16,0},{144,1},{18,2},{146,3},{20,4},{148,5},{22,6},{150,7},{24,8}... | collective-permute-start | bytes 294920 | tf_op jit(solution)/shard_map/ppermute | solution.py:44
  12.2 9.4 %collective-permute-start.7 = (bf16[128,384]{1,0:T(8,128)(2,1)}, bf16[128,384]{1,0:T(8,128)(2,1)S(1)}, u32[]{:S(2)}, u32[]{:S(2)}) collective-permute-start(bf16[128,384]{1,0:T(8,128)(2,1)} %param.13), channel_id=1, source_target_pairs={{24,0},{152,1},{26,2},{154,3},{28,4},{156,5},{30,6},{158,7},{0,8},... | collective-permute-start | bytes 294920 | tf_op jit(solution)/shard_map/ppermute | solution.py:44
  14.3 4.5 %collective-permute-start = (f32[8]{0:T(128)S(1)}, f32[8]{0:T(128)S(1)}, u32[]{:S(2)}, u32[]{:S(2)}) collective-permute-start(f32[8]{0:T(128)S(1)} %select_reduce_fusion.1), channel_id=1, source_target_pairs={{1,0},{0,1},{3,2},{2,3},{5,4},{4,5},{7,6},{6,7},{9,8},{8,9},{11,10... | collective-permute-start | bytes 104 | tf_op jit(solution)/shard_map/ppermute | solution.py:59
  21.6 80.1 %all-to-all-start = ((bf16[16,768,128]{2,1,0:T(8,128)(2,1)}), bf16[16,768,128]{2,1,0:T(8,128)(2,1)}, u32[]{:S(2)}, u32[]{:S(2)}) async-start(bf16[16,768,128]{2,1,0:T(8,128)(2,1)} %pack.1), calls=%async_computation | async-start | bytes 6291456 | tf_op jit(solution)/shard_map/all_to_all | solution.py:393
  29.1 4.4 %collective-permute-start.1 = (f32[8]{0:T(128)S(1)}, f32[8]{0:T(128)S(1)}, u32[]{:S(2)}, u32[]{:S(2)}) collective-permute-start(f32[8]{0:T(128)S(1)} %add.45), channel_id=1, source_target_pairs={{4,0},{5,1},{6,2},{7,3},{0,4},{1,5},{2,6},{3,7},{12,8},{13,9},{14,... | collective-permute-start | bytes 104 | tf_op jit(solution)/shard_map/ppermute | solution.py:54
  36.9 16.7 %collective-permute-start.10 = (bf16[512,384]{1,0:T(8,128)(2,1)S(1)}, bf16[512,384]{1,0:T(8,128)(2,1)S(1)}, u32[]{:S(2)}, u32[]{:S(2)}) collective-permute-start(bf16[512,384]{1,0:T(8,128)(2,1)S(1)} %constant_dynamic-update-slice_fusion), channel_id=1, source_target_pairs={{64,0},{72,8},{80,16},{88,24},{96,32},{104,40},{112,48},{120,56},{... | collective-permute-start | bytes 1179656 | tf_op jit(solution)/shard_map/ppermute | solution.py:29
  39.7 27.5 %collective-permute-start.11 = (bf16[512,384]{1,0:T(8,128)(2,1)S(1)}, bf16[512,384]{1,0:T(8,128)(2,1)S(1)}, u32[]{:S(2)}, u32[]{:S(2)}) collective-permute-start(bf16[512,384]{1,0:T(8,128)(2,1)S(1)} %constant_dynamic-update-slice_fusion), channel_id=1, source_target_pairs={{96,0},{104,8},{112,16},{120,24},{0,32},{8,40},{16,48},{24,56},{32... | collective-permute-start | bytes 1179656 | tf_op jit(solution)/shard_map/ppermute | solution.py:29
  40.0 28.7 %collective-permute-start.8 = (bf16[512,384]{1,0:T(8,128)(2,1)S(1)}, bf16[512,384]{1,0:T(8,128)(2,1)S(1)}, u32[]{:S(2)}, u32[]{:S(2)}) collective-permute-start(bf16[512,384]{1,0:T(8,128)(2,1)S(1)} %constant_dynamic-update-slice_fusion), channel_id=1, source_target_pairs={{32,0},{40,8},{48,16},{56,24},{64,32},{72,40},{80,48},{88,56},{96,... | collective-permute-start | bytes 1179656 | tf_op jit(solution)/shard_map/ppermute | solution.py:29
  67.3 20.1 %collective-permute-start.12 = (bf16[1024,384]{1,0:T(8,128)(2,1)S(1)}, bf16[1024,384]{1,0:T(8,128)(2,1)}, u32[]{:S(2)}, u32[]{:S(2)}) collective-permute-start(bf16[1024,384]{1,0:T(8,128)(2,1)S(1)} %constant_dynamic-update-slice_fusion.6.rest_1_), channel_id=1, source_target_pairs={{6,0},{7,1},{0,2},{1,3},{2,4},{3,5},{4,6},{5,7},{14,8},{15,9},{8,1... | collective-permute-start | bytes 2359304 | tf_op jit(solution)/shard_map/ppermute | solution.py:54
  68.8 19.7 %collective-permute-start.9 = (bf16[1024,384]{1,0:T(8,128)(2,1)S(1)}, bf16[1024,384]{1,0:T(8,128)(2,1)S(1)}, u32[]{:S(2)}, u32[]{:S(2)}) collective-permute-start(bf16[1024,384]{1,0:T(8,128)(2,1)S(1)} %constant_dynamic-update-slice_fusion.4.rest_0_), channel_id=1, source_target_pairs={{2,0},{3,1},{4,2},{5,3},{6,4},{7,5},{0,6},{1,7},{10,8},{11,9},{12,... | collective-permute-start | bytes 2359304 | tf_op jit(solution)/shard_map/ppermute | solution.py:54
  70.3 18.3 %collective-permute-start.14 = (bf16[1024,384]{1,0:T(8,128)(2,1)S(1)}, bf16[1024,384]{1,0:T(8,128)(2,1)S(1)}, u32[]{:S(2)}, u32[]{:S(2)}) collective-permute-start(bf16[1024,384]{1,0:T(8,128)(2,1)S(1)} %constant_dynamic-update-slice_fusion.6.rest_1_), channel_id=1, source_target_pairs={{0,128},{128,0},{1,129},{129,1},{2,130},{130,2},{3,131},{131,3},{4... | collective-permute-start | bytes 2359304 | tf_op jit(solution)/shard_map/ppermute | solution.py:63
  71.3 18.2 %collective-permute-start.13 = (bf16[1024,384]{1,0:T(8,128)(2,1)S(1)}, bf16[1024,384]{1,0:T(8,128)(2,1)}, u32[]{:S(2)}, u32[]{:S(2)}) collective-permute-start(bf16[1024,384]{1,0:T(8,128)(2,1)S(1)} %constant_dynamic-update-slice_fusion.4.rest_0_), channel_id=1, source_target_pairs={{0,128},{128,0},{1,129},{129,1},{2,130},{130,2},{3,131},{131,3},{4... | collective-permute-start | bytes 2359304 | tf_op jit(solution)/shard_map/ppermute | solution.py:63
  71.3 42.1 %collective-permute-start.15 = (bf16[1024,384]{1,0:T(8,128)(2,1)S(1)}, bf16[1024,384]{1,0:T(8,128)(2,1)}, u32[]{:S(2)}, u32[]{:S(2)}) collective-permute-start(bf16[1024,384]{1,0:T(8,128)(2,1)S(1)} %constant_dynamic-update-slice_fusion.6.rest_1_), channel_id=1, source_target_pairs={{2,0},{3,1},{4,2},{5,3},{6,4},{7,5},{0,6},{1,7},{10,8},{11,9},{12,... | collective-permute-start | bytes 2359304 | tf_op jit(solution)/shard_map/ppermute | solution.py:54
  87.4 26.0 %collective-permute-start.16 = (bf16[1024,384]{1,0:T(8,128)(2,1)S(1)}, bf16[1024,384]{1,0:T(8,128)(2,1)}, u32[]{:S(2)}, u32[]{:S(2)}) collective-permute-start(bf16[1024,384]{1,0:T(8,128)(2,1)S(1)} %constant_dynamic-update-slice_fusion.4.rest_0_), channel_id=1, source_target_pairs={{6,0},{7,1},{0,2},{1,3},{2,4},{3,5},{4,6},{5,7},{14,8},{15,9},{8,1... | collective-permute-start | bytes 2359304 | tf_op jit(solution)/shard_map/ppermute | solution.py:54
  101.8 24.3 %all-to-all-start.1 = ((bf16[16,128,128]{2,1,0:T(8,128)(2,1)}), bf16[16,128,128]{2,1,0:T(8,128)(2,1)}, u32[]{:S(2)}, u32[]{:S(2)}) async-start(bf16[16,128,128]{2,1,0:T(8,128)(2,1)} %pack_queries.1), calls=%async_computation.1 | async-start | bytes 1048576 | tf_op jit(solution)/shard_map/all_to_all | solution.py:393
  110.4 27.0 %collective-permute-start.18 = (bf16[1024,384]{1,0:T(8,128)(2,1)}, bf16[1024,384]{1,0:T(8,128)(2,1)}, u32[]{:S(2)}, u32[]{:S(2)}) collective-permute-start(bf16[1024,384]{1,0:T(8,128)(2,1)} %collective-permute-done.12.rest_5_), channel_id=1, source_target_pairs={{6,0},{7,1},{0,2},{1,3},{2,4},{3,5},{4,6},{5,7},{14,8},{15,9},{8,1... | collective-permute-start | bytes 2359304 | tf_op jit(solution)/shard_map/ppermute | solution.py:54
  112.1 25.3 %collective-permute-start.17 = (bf16[1024,384]{1,0:T(8,128)(2,1)S(1)}, bf16[1024,384]{1,0:T(8,128)(2,1)}, u32[]{:S(2)}, u32[]{:S(2)}) collective-permute-start(bf16[1024,384]{1,0:T(8,128)(2,1)S(1)} %collective-permute-done.9.rest_2_), channel_id=1, source_target_pairs={{2,0},{3,1},{4,2},{5,3},{6,4},{7,5},{0,6},{1,7},{10,8},{11,9},{12,... | collective-permute-start | bytes 2359304 | tf_op jit(solution)/shard_map/ppermute | solution.py:54
  137.4 30.0 %all-to-all-start.2 = ((bf16[16,256,128]{2,1,0:T(8,128)(2,1)}), bf16[16,256,128]{2,1,0:T(8,128)(2,1)}, u32[]{:S(2)}, u32[]{:S(2)}) async-start(bf16[16,256,128]{2,1,0:T(8,128)(2,1)} %attention1.1), calls=%async_computation.2 | async-start | bytes 2097152 | tf_op jit(solution)/shard_map/all_to_all | solution.py:393
  144.9 4.3 %collective-permute-start.22 = (bf16[1024,384]{1,0:T(8,128)(2,1)}, bf16[1024,384]{1,0:T(8,128)(2,1)}, u32[]{:S(2)}, u32[]{:S(2)}) collective-permute-start(bf16[1024,384]{1,0:T(8,128)(2,1)} %collective-permute-done.12.rest_5_), channel_id=1, source_target_pairs={{0,128},{128,0},{1,129},{129,1},{2,130},{130,2},{3,131},{131,3},{4... | collective-permute-start | bytes 2359304 | tf_op jit(solution)/shard_map/ppermute | solution.py:63
  147.0 20.3 %collective-permute-start.19 = (bf16[1024,384]{1,0:T(8,128)(2,1)S(1)}, bf16[1024,384]{1,0:T(8,128)(2,1)}, u32[]{:S(2)}, u32[]{:S(2)}) collective-permute-start(bf16[1024,384]{1,0:T(8,128)(2,1)S(1)} %collective-permute-done.9.rest_2_), channel_id=1, source_target_pairs={{0,128},{128,0},{1,129},{129,1},{2,130},{130,2},{3,131},{131,3},{4... | collective-permute-start | bytes 2359304 | tf_op jit(solution)/shard_map/ppermute | solution.py:63
  147.2 20.2 %collective-permute-start.20 = (bf16[1024,384]{1,0:T(8,128)(2,1)}, bf16[1024,384]{1,0:T(8,128)(2,1)}, u32[]{:S(2)}, u32[]{:S(2)}) collective-permute-start(bf16[1024,384]{1,0:T(8,128)(2,1)} %collective-permute-done.15.rest_3_), channel_id=1, source_target_pairs={{0,128},{128,0},{1,129},{129,1},{2,130},{130,2},{3,131},{131,3},{4... | collective-permute-start | bytes 2359304 | tf_op jit(solution)/shard_map/ppermute | solution.py:63
  147.6 19.7 %collective-permute-start.21 = (bf16[1024,384]{1,0:T(8,128)(2,1)}, bf16[1024,384]{1,0:T(8,128)(2,1)}, u32[]{:S(2)}, u32[]{:S(2)}) collective-permute-start(bf16[1024,384]{1,0:T(8,128)(2,1)} %collective-permute-done.16.rest_4_), channel_id=1, source_target_pairs={{0,128},{128,0},{1,129},{129,1},{2,130},{130,2},{3,131},{131,3},{4... | collective-permute-start | bytes 2359304 | tf_op jit(solution)/shard_map/ppermute | solution.py:63
  147.7 19.6 %collective-permute-start.24 = (bf16[1024,384]{1,0:T(8,128)(2,1)}, bf16[1024,384]{1,0:T(8,128)(2,1)}, u32[]{:S(2)}, u32[]{:S(2)}) collective-permute-start(bf16[1024,384]{1,0:T(8,128)(2,1)} %collective-permute-done.18.rest_7_), channel_id=1, source_target_pairs={{0,128},{128,0},{1,129},{129,1},{2,130},{130,2},{3,131},{131,3},{4... | collective-permute-start | bytes 2359304 | tf_op jit(solution)/shard_map/ppermute | solution.py:63
  149.3 18.1 %collective-permute-start.23 = (bf16[1024,384]{1,0:T(8,128)(2,1)}, bf16[1024,384]{1,0:T(8,128)(2,1)}, u32[]{:S(2)}, u32[]{:S(2)}) collective-permute-start(bf16[1024,384]{1,0:T(8,128)(2,1)} %collective-permute-done.17.rest_6_), channel_id=1, source_target_pairs={{0,128},{128,0},{1,129},{129,1},{2,130},{130,2},{3,131},{131,3},{4... | collective-permute-start | bytes 2359304 | tf_op jit(solution)/shard_map/ppermute | solution.py:63
  178.2 5.1 %collective-permute-start.25 = (f32[64,256]{1,0:T(8,128)S(1)}, f32[64,256]{1,0:T(8,128)S(1)}, u32[]{:S(2)}, u32[]{:S(2)}) collective-permute-start(f32[64,256]{1,0:T(8,128)S(1)} %get-tuple-element.19.own_ref), channel_id=1, source_target_pairs={{0,128},{128,0},{1,129},{129,1},{2,130},{130,2},{3,131},{131,3},{4... | collective-permute-start | bytes 196616 | tf_op jit(solution)/shard_map/ppermute | solution.py:63
  205.5 7.3 %collective-permute-start.27 = (f32[40,384]{1,0:T(8,128)}, f32[40,384]{1,0:T(8,128)S(1)}, u32[]{:S(2)}, u32[]{:S(2)}) collective-permute-start(f32[40,384]{1,0:T(8,128)} %fold.1), channel_id=1, source_target_pairs={{16,0},{24,8},{0,16},{8,24},{48,32},{56,40},{32,48},{40,56},{80,64... | collective-permute-start | bytes 184328 | tf_op jit(solution)/shard_map/ppermute | solution.py:49
  205.7 7.1 %collective-permute-start.28 = (f32[40,384]{1,0:T(8,128)}, f32[40,384]{1,0:T(8,128)S(1)}, u32[]{:S(2)}, u32[]{:S(2)}) collective-permute-start(f32[40,384]{1,0:T(8,128)} %fold.1), channel_id=1, source_target_pairs={{8,0},{16,8},{24,16},{0,24},{40,32},{48,40},{56,48},{32,56},{72,64... | collective-permute-start | bytes 184328 | tf_op jit(solution)/shard_map/ppermute | solution.py:49
  208.1 5.6 %collective-permute-start.29 = (f32[40,384]{1,0:T(8,128)}, f32[40,384]{1,0:T(8,128)S(1)}, u32[]{:S(2)}, u32[]{:S(2)}) collective-permute-start(f32[40,384]{1,0:T(8,128)} %fold.1), channel_id=1, source_target_pairs={{24,0},{0,8},{8,16},{16,24},{56,32},{32,40},{40,48},{48,56},{88,64... | collective-permute-start | bytes 184328 | tf_op jit(solution)/shard_map/ppermute | solution.py:49
  214.6 4.7 %collective-permute-start.30 = (f32[40,384]{1,0:T(8,128)S(1)}, f32[40,384]{1,0:T(8,128)S(1)}, u32[]{:S(2)}, u32[]{:S(2)}) collective-permute-start(f32[40,384]{1,0:T(8,128)S(1)} %add_add_fusion.1), channel_id=1, source_target_pairs={{64,0},{72,8},{80,16},{88,24},{96,32},{104,40},{112,48},{120,56},{... | collective-permute-start | bytes 184328 | tf_op jit(solution)/shard_map/ppermute | solution.py:29
  222.2 5.8 %collective-permute-start.33 = (f32[40,384]{1,0:T(8,128)S(1)}, f32[40,384]{1,0:T(8,128)S(1)}, u32[]{:S(2)}, u32[]{:S(2)}) collective-permute-start(f32[40,384]{1,0:T(8,128)S(1)} %add_add_fusion), channel_id=1, source_target_pairs={{0,128},{128,0},{1,129},{129,1},{2,130},{130,2},{3,131},{131,3},{4... | collective-permute-start | bytes 184328 | tf_op jit(solution)/shard_map/ppermute | solution.py:63
  (16 other events, 268.2 us)
